TPU v7x, 512 devices: a whole 4x8x8 slice. The times are simulated.
512 devices in a mesh: seq: 16 (over y_hi, x), dp: 32 (over z, y_lo, core).
Axes of the slice: x: 4, y: 8 (y_hi: 4, y_lo: 2; y = y_hi * 2 + y_lo), z: 8, core: 2. Of those that a mesh axis runs over, the one named last changes fastest.
Arguments:
- queries: bfloat16 [32, 2048, 2048], P('dp', 'seq'), may hold values from -96 to 96
- pool: bfloat16 [32, 96, 128, 896], P('dp', 'seq'), may hold values from -8 to 8
- slots: int32 [32, 32, 2], P('dp', 'seq'), may hold values from 0 to 5
- key_weight: bfloat16 [896, 2048], P('dp'), may hold values from -0.141 to 0.141
- value_weight: bfloat16 [896, 2048], P('dp'), may hold values from -0.1875 to 0.1875
- cotangent: bfloat16 [32, 2048, 2048], P('dp', 'seq'), may hold values from -6 to 6
Outputs:
- attended: bfloat16 [32, 2048, 2048], P('dp', 'seq')
- query_grad: bfloat16 [32, 2048, 2048], P('dp', 'seq')
- value_weight_grad: float32 [896, 2048], P('dp')
All inputs are finite; a program needn't handle non-finite values.
Results may differ from a plain program's by a relative error of at most 0.039.
Values may be sent and summed in bfloat16 or wider, within the bound.
No kernel may reach another device: no remote copies, remote signals or barrier semaphores. Data moves between devices by JAX's collectives and lax.ppermute only.
A program may use at most 64 MiB of HBM per device.

v0:
```python
import math

import jax
import jax.numpy as jnp
from jax import lax
from jax.sharding import PartitionSpec as P

HEADS = 16
HEAD_DIM = 128
BLOCK = 64


def shifted(block, axis, distance):
    devices = range(lax.axis_size(axis))
    route = [(i - distance, i) for i in devices if i - distance in devices]
    return lax.ppermute(block, axis, route)


def pick_rows(pool, slots):
    pool_table = pool[0]
    chosen = jnp.take(pool_table, slots[0].reshape(-1), axis=0)
    return chosen.reshape(slots.shape[1], -1, pool_table.shape[-1])


def project_rows(enc_rows, key_weight, value_weight):
    key_full, value_full = (
        lax.all_gather(key_weight, "dp", axis=0, tiled=True),
        lax.all_gather(value_weight, "dp", axis=0, tiled=True),
    )
    key_rows = jnp.dot(enc_rows, key_full, preferred_element_type=jnp.float32)
    value_rows = jnp.dot(enc_rows, value_full, preferred_element_type=jnp.float32)
    return (key_rows.astype(jnp.bfloat16), value_rows.astype(jnp.bfloat16))


def body(queries, pool, slots, key_weight, value_weight, cotangent):
    local_rows = pick_rows(pool, slots)
    block_count, key_span, enc_width = local_rows.shape
    arrived = shifted(local_rows[block_count - 1], "seq", 1)
    earlier = jnp.concatenate([arrived[None], local_rows[: block_count - 1]], axis=0)
    key_rows, value_rows = project_rows(earlier.reshape(-1, enc_width), key_weight, value_weight)
    key_rows = key_rows.reshape(block_count, key_span, -1)
    value_rows = value_rows.reshape(block_count, key_span, -1)
    score_scale = 1.0 / math.sqrt(HEAD_DIM)
    key_heads = key_rows.reshape(block_count, key_span, HEADS, HEAD_DIM)
    value_heads = value_rows.reshape(block_count, key_span, HEADS, HEAD_DIM)
    query_heads = queries.reshape(block_count, BLOCK, HEADS, HEAD_DIM)
    out_grad = cotangent.reshape(block_count, BLOCK, HEADS, HEAD_DIM)
    scores = (
        jnp.einsum("cqhd,ckhd->chqk", query_heads, key_heads, preferred_element_type=jnp.float32)
        * score_scale
    )
    attn_probs = jax.nn.softmax(scores, axis=-1)
    probs_low = attn_probs.astype(jnp.bfloat16)
    attended = jnp.einsum(
        "chqk,ckhd->cqhd", probs_low, value_heads, preferred_element_type=jnp.float32
    ).astype(jnp.bfloat16)
    prob_grad = jnp.einsum(
        "cqhd,ckhd->chqk", out_grad, value_heads, preferred_element_type=jnp.float32
    )
    row_total = jnp.einsum("cqhd,cqhd->chq", out_grad, attended, preferred_element_type=jnp.float32)
    score_grad = (score_scale * attn_probs * (prob_grad - row_total[..., None])).astype(
        jnp.bfloat16
    )
    query_grad = jnp.einsum(
        "chqk,ckhd->cqhd", score_grad, key_heads, preferred_element_type=jnp.float32
    ).astype(jnp.bfloat16)
    value_grad = jnp.einsum(
        "chqk,cqhd->ckhd", probs_low, out_grad, preferred_element_type=jnp.float32
    ).astype(jnp.bfloat16)
    grad_term = jnp.einsum(
        "me,mh->eh",
        earlier.reshape(-1, enc_width),
        value_grad.reshape(block_count * key_span, -1),
        preferred_element_type=jnp.float32,
    )
    grad_shard = lax.psum_scatter(
        grad_term.astype(jnp.bfloat16), "dp", scatter_dimension=0, tiled=True
    )
    weight_grad = lax.psum(grad_shard, "seq").astype(jnp.float32)
    return (attended.reshape(queries.shape), query_grad.reshape(queries.shape), weight_grad)


def solution(mesh):
    return jax.shard_map(
        body,
        mesh=mesh,
        in_specs=(
            P("dp", "seq", None),
            P("dp", "seq", None, None),
            P("dp", "seq", None),
            P("dp", None),
            P("dp", None),
            P("dp", "seq", None),
        ),
        out_specs=(P("dp", "seq", None), P("dp", "seq", None), P("dp", None)),
        check_vma=False,
    )
```

profile of v0, /device:TPU:22, one launch (start us, length us, event | category | flops | bytes accessed | tf_op | source)
XLA Modules:
  0.0 418.3 jit_solution(13418757251322171441)
XLA Ops:
  7.2 0.0 all-gather.7.cloned.1.call-start
  7.2 0.7 all-gather.7.cloned.1.call-update
  7.9 0.0 all-gather.5.cloned.1.call-start
  8.0 0.7 all-gather.5.cloned.1.call-update
  8.7 0.0 all-reduce.4.cloned.1.call-start
  8.7 0.8 reshape_squeeze.6
  9.5 0.8 reshape_squeeze.5
  10.3 0.7 gather_fusion
  11.0 0.2 broadcast_select_fusion
  11.2 0.1 fusion.54
  11.2 5.8 %collective-permute-start = (bf16[256,896]{1,0:T(8,128)(2,1)S(1)}, bf16[256,896]{1,0:T(8,128)(2,1)S(1)}, u32[]{:S(2)}, u32[]{:S(2)}) collective-permute-start(bf16[256,896]{1,0:T(8,128)(2,1)S(1)} %bitcast.108), channel_id=1, source_target_pairs={{0,32},{32,64},{64,96},{96,128},{128,160},{160,192},{192,224},{224... | collective-permute-start | bytes 1376264 | tf_op jit(solution)/shard_map/ppermute | solution.py:16
  17.0 0.9 copy.40
  17.9 0.9 copy.42
  18.8 1.3 dynamic-slice.4
  20.7 18.1 %collective-permute-done = bf16[256,896]{1,0:T(8,128)(2,1)S(1)} collective-permute-done((bf16[256,896]{1,0:T(8,128)(2,1)S(1)}, bf16[256,896]{1,0:T(8,128)(2,1)S(1)}, u32[]{:S(2)}, u32[]{:S(2)}) %collective-permute-start) | collective-permute-done | bytes 458784 | tf_op jit(solution)/shard_map/ppermute | solution.py:16
  38.8 0.1 pad_maximum_fusion
  38.9 52.7 %all-gather.7.cloned.1.call-done = bf16[32,28,2048]{2,1,0:T(8,128)(2,1)} async-done(((bf16[1,28,2048]{2,1,0:T(8,128)(2,1)}), bf16[32,28,2048]{2,1,0:T(8,128)(2,1)}) %all-gather.7.cloned.1.call-update) | async-done | bytes 3670032 | tf_op jit(solution)/shard_map/all_gather | solution.py:27
  91.6 5.8 %reshape.83 = bf16[896,2048]{1,0:T(8,128)(2,1)} reshape(bf16[32,28,2048]{2,1,0:T(8,128)(2,1)} %all-gather.7.cloned.1.call-done) | data formatting | bytes 7340032
  97.4 4.4 %fusion.19 = bf16[64,8,16,128]{3,1,2,0:T(8,128)(2,1)S(1)} fusion(bf16[512,896]{1,0:T(8,128)(2,1)S(1)} %bitcast.102, bf16[896,2048]{1,0:T(8,128)(2,1)} %reshape.83), kind=kOutput, calls=%fused_computation.24 | convolution fusion | flops 1880096768 | bytes 6684672 | tf_op jit(solution)/shard_map/dot_general | solution.py:30
  101.8 0.6 copy.39
  102.4 0.4 copy-done.2
  102.8 0.8 fusion.16
  103.7 2.0 fusion.55
  105.7 8.0 %convert_bitcast_fusion = bf16[2,256,16,128]{3,1,2,0:T(8,128)(2,1)} fusion(bf16[2,64,16,128]{3,2,1,0:T(8,128)(2,1)} %bitcast.94, f32[2,16,64]{2,1,0:T(8,128)S(1)} %get-tuple-element.5, f32[2,16,256,64]{2,3,1,0:T(8,128)} %copy-done.1), kind=kOutput, calls=%fused_computation.13 | convolution fusion | flops 137890048 | bytes 4726784 | tf_op jit(solution)/shard_map/chqk,cqhd->ckhd/dot_general | solution.py:67
  113.7 3.1 copy.31
  116.8 3.9 convolution_convert_fusion
  120.7 80.0 %fusion = bf16[32,2048]{1,0:T(8,128)(2,1)} fusion(bf16[896,2048]{1,0:T(8,128)(2,1)} %convolution_convert_fusion), kind=kCustom, calls=%all-reduce-scatter | all-reduce-scatter fusion | flops 2097153 | bytes 3803136
  200.8 1.6 slice.17
  202.3 1.9 collective-permute-start.3
  204.3 1.9 collective-permute-start.2
  206.2 1.9 collective-permute-start.1
  208.2 5.8 %reshape.81 = bf16[896,2048]{1,0:T(8,128)(2,1)} reshape(bf16[32,28,2048]{2,1,0:T(8,128)(2,1)} %all-gather.5.cloned.1.call-done) | data formatting | bytes 7340032
  214.0 4.7 %fusion.18 = bf16[64,8,16,128]{3,1,2,0:T(8,128)(2,1)S(1)} fusion(bf16[512,896]{1,0:T(8,128)(2,1)} %bitcast.103, bf16[896,2048]{1,0:T(8,128)(2,1)} %reshape.81), kind=kOutput, calls=%fused_computation.23 | convolution fusion | flops 1880096768 | bytes 6684672 | tf_op jit(solution)/shard_map/dot_general | solution.py:31
  218.7 2.0 copy.41
  220.6 7.7 %bitcast_convert_fusion = (f32[2,16,64,128]{3,2,1,0:T(8,128)}, bf16[2,16,128,64]{2,3,1,0:T(8,128)(2,1)}) fusion(bf16[2,256,16,128]{3,2,1,0:T(8,128)(2,1)} %bitcast.98, f32[2,16,64]{2,1,0:T(8,128)S(1)} %get-tuple-element.5, f32[2,16,256,64]{2,3,1,0:T(8,128)} %copy-done.1), kind=kOutput, calls=%fused_computation.36 | convolution fusion | flops 137365760 | bytes 5775360 | tf_op jit(solution)/shard_map/chqk,ckhd->cqhd/dot_general | solution.py:54
  228.3 1.9 collective-permute-start.4
  230.2 2.0 multiply_reduce_fusion
  232.3 0.7 copy.38
  233.0 8.3 %concatenate.4 = bf16[156,2048]{1,0:T(8,128)(2,1)} concatenate(bf16[28,2048]{1,0:T(8,128)(2,1)} %collective-permute-done.4, bf16[32,2048]{1,0:T(8,128)(2,1)} %collective-permute-done.3, bf16[32,2048]{1,0:T(8,128)(2,1)} %collective-permute-done.2, bf16[32,2048]{1,0:T(8,128)(2,1)} %collective-permute-done.1, bf16[32,2048]{1,0:T(8,128)(2,1)} %fusion), dimensions={0} | concatenate | bytes 1277952
  241.2 1.6 constant_dynamic-slice_fusion
  242.8 0.0 all-reduce.4.cloned.1.call-update
  242.9 4.9 %fusion.28 = bf16[2,64,16,128]{3,1,2,0:T(8,128)(2,1)} fusion(bf16[2,256,16,128]{3,2,1,0:T(8,128)(2,1)S(1)} %bitcast.93, bf16[2,256,16,128]{3,2,1,0:T(8,128)(2,1)} %bitcast.99, f32[2,16,64]{2,1,0:T(8,128)} %copy.38, f32[2,16,64,256]{3,2,1,0:T(8,128)} %get-tuple-element.6, f32[2,16,64]{2,1,0:T(8,128)S(1)} %get-tuple-element.5, ...), kind=kOutput, calls=%fused_computation.27 | convolution fusion | flops 271319040 | bytes 7356416 | tf_op jit(solution)/shard_map/chqk,ckhd->cqhd/dot_general | solution.py:64
  247.8 1.4 copy.25
  249.2 1.0 reshape.68
  250.3 0.3 copy.29
  250.6 1.0 reshape.70
  251.6 158.5 %all-reduce.4.cloned.1.call-done = bf16[28,2048]{1,0:T(8,128)(2,1)} async-done(((bf16[28,2048]{1,0:T(8,128)(2,1)}), bf16[28,2048]{1,0:T(8,128)(2,1)}) %all-reduce.4.cloned.1.call-update) | async-done | bytes 114704 | tf_op jit(solution)/shard_map/psum | solution.py:79
  410.2 1.6 convert_element_type.47
  (23 shorter events, 0.1 us)
Async XLA Ops:
  7.2 3.1 copy-start
  7.2 84.4 %all-gather.7.cloned.1.call-start = ((), (), s32[]{:S(2)}) async-start(), calls=%async_computation.2 | async-start | bytes 4325376 | tf_op jit(solution)/shard_map/all_gather | solution.py:27
  7.9 200.3 %all-gather.5.cloned.1.call-start = ((), (), s32[]{:S(2)}) async-start(), calls=%async_computation.1 | async-start | bytes 4325376 | tf_op jit(solution)/shard_map/all_gather | solution.py:28
  8.7 401.5 %all-reduce.4.cloned.1.call-start = ((), (), s32[]{:S(2)}) async-start(), calls=%async_computation | async-start | bytes 262144 | tf_op jit(solution)/shard_map/psum | solution.py:79
  11.0 6.0 %copy-start.5 = (bf16[1,128,2048]{2,1,0:T(8,128)(2,1)S(1)}, bf16[1,128,2048]{2,1,0:T(8,128)(2,1)}, u32[]{:S(2)}) copy-start(bf16[1,128,2048]{2,1,0:T(8,128)(2,1)} %param.6) | copy-start | bytes 1572868
  11.0 6.9 %copy-start.6 = (bf16[1,128,2048]{2,1,0:T(8,128)(2,1)S(1)}, bf16[1,128,2048]{2,1,0:T(8,128)(2,1)}, u32[]{:S(2)}) copy-start(bf16[1,128,2048]{2,1,0:T(8,128)(2,1)} %param.11) | copy-start | bytes 1572868
  11.2 27.6 %collective-permute-start = (bf16[256,896]{1,0:T(8,128)(2,1)S(1)}, bf16[256,896]{1,0:T(8,128)(2,1)S(1)}, u32[]{:S(2)}, u32[]{:S(2)}) collective-permute-start(bf16[256,896]{1,0:T(8,128)(2,1)S(1)} %bitcast.108), channel_id=1, source_target_pairs={{0,32},{32,64},{64,96},{96,128},{128,160},{160,192},{192,224},{224... | collective-permute-start | bytes 1376264 | tf_op jit(solution)/shard_map/ppermute | solution.py:16
  38.9 58.5 %copy-start.3 = (bf16[2,256,896]{2,1,0:T(8,128)(2,1)}, bf16[2,256,896]{2,1,0:T(8,128)(2,1)S(1)}, u32[]{:S(2)}) copy-start(bf16[2,256,896]{2,1,0:T(8,128)(2,1)S(1)} %pad_maximum_fusion) | copy-start | bytes 2752516
  101.8 1.0 copy-start.2
  103.6 2.0 copy-start.1
  113.7 3.1 copy-start.4
  202.3 30.6 %collective-permute-start.3 = (bf16[32,2048]{1,0:T(8,128)(2,1)}, bf16[32,2048]{1,0:T(8,128)(2,1)}, u32[]{:S(2)}, u32[]{:S(2)}) collective-permute-start(bf16[32,2048]{1,0:T(8,128)(2,1)} %fusion), channel_id=1, source_target_pairs={{0,3},{1,4},{2,5},{3,6},{4,7},{5,8},{6,9},{7,10},{8,11},{9,12},{10... | collective-permute-start | bytes 393224
  204.3 28.7 %collective-permute-start.2 = (bf16[32,2048]{1,0:T(8,128)(2,1)}, bf16[32,2048]{1,0:T(8,128)(2,1)}, u32[]{:S(2)}, u32[]{:S(2)}) collective-permute-start(bf16[32,2048]{1,0:T(8,128)(2,1)} %fusion), channel_id=1, source_target_pairs={{0,2},{1,3},{2,4},{3,5},{4,6},{5,7},{6,8},{7,9},{8,10},{9,11},{10,... | collective-permute-start | bytes 393224
  206.2 26.7 %collective-permute-start.1 = (bf16[32,2048]{1,0:T(8,128)(2,1)}, bf16[32,2048]{1,0:T(8,128)(2,1)}, u32[]{:S(2)}, u32[]{:S(2)}) collective-permute-start(bf16[32,2048]{1,0:T(8,128)(2,1)} %fusion), channel_id=1, source_target_pairs={{0,1},{1,2},{2,3},{3,4},{4,5},{5,6},{6,7},{7,8},{8,9},{9,10},{10,1... | collective-permute-start | bytes 393224
  228.3 4.6 %collective-permute-start.4 = (bf16[28,2048]{1,0:T(8,128)(2,1)}, bf16[28,2048]{1,0:T(8,128)(2,1)}, u32[]{:S(2)}, u32[]{:S(2)}) collective-permute-start(bf16[28,2048]{1,0:T(8,128)(2,1)} %slice.17), channel_id=1, source_target_pairs={{0,4},{1,5},{2,6},{3,7},{4,8},{5,9},{6,10},{7,11},{8,12},{9,13},{1... | collective-permute-start | bytes 344072
  247.8 2.5 copy-start.7
Sparse Core Ops, SparseCore 0:
  10.2 81.3 all-gather.6
  93.7 71.7 all-gather.4
  243.0 167.1 all-reduce.3
where the time goes:
time: 420 us; the launch traced here: 418 us
  waiting for transfers between devices  231 us (55%)
  blocking collectives  80 us (19%)
  local copies, waits for them, and re-layouts  39 us (9%)
  matrix products  34.4 us (8%)
  between operations  14.6 us (3%)
  starting transfers between devices  13.6 us (3%)
  other arithmetic  5.95 us (1%)
    psum x1, waiting for transfers between devices, body(): weight_grad = lax.psum(grad_shard, 'seq').astype(jnp.float32)  159 us
    unnamed x1, blocking collectives  80 us
    all_gather x1, waiting for transfers between devices, project_rows(): lax.all_gather(key_weight, 'dp', axis=0, tiled=True)  52.7 us
    unnamed x26, local copies, waits for them, and re-layouts  29.2 us
    ppermute x1, waiting for transfers between devices, shifted(): return lax.ppermute(block, axis, route)  18.1 us
  transfers between devices with their start and end apart: 8, of which 3 were waited for; matrix products, arithmetic and copies ran while one was open for 35% of the time, Pallas kernels for 0%

commit v1 on v0

v1 whole, which is shorter than its diff:
```python
import math

import jax
import jax.numpy as jnp
from jax import lax
from jax.experimental import pallas as pl
from jax.experimental.pallas import tpu as pltpu
from jax.sharding import Mesh
from jax.sharding import PartitionSpec as P

HEAD_DIM = 128
BLOCK = 64
SPAN = 256
SCALE = 1.0 / math.sqrt(HEAD_DIM)

AXES = ("yhi", "xh", "xp", "z", "ylo", "core")
SIZES = (4, 2, 2, 8, 2, 2)
SEQ = ("yhi", "xh", "xp")
DP = ("z", "ylo", "core")
N_Z = 8
VMEM = 44 * 1024 * 1024


def route(dx, dy, flip=False):
    pairs = []
    for i in range(math.prod(SIZES)):
        rest, core = divmod(i, 2)
        rest, ylo = divmod(rest, 2)
        rest, z = divmod(rest, N_Z)
        yhi, x = divmod(rest, 4)
        y = (2 * yhi + ylo + dy) % 8
        x = (x + dx) % 4
        core = 1 - core if flip else core
        there = ((((y // 2) * 4 + x) * N_Z + z) * 2 + y % 2) * 2 + core
        pairs.append((i, there))
    return pairs


def send(value, dx, dy, flip=False):
    return lax.ppermute(value, AXES, route(dx, dy, flip))


def after(value, token):
    return lax.optimization_barrier((value, token))[0]


def swap(value):
    return send(value, 0, 0, True)


def next_group(rows):
    n = 16
    return lax.ppermute(rows, SEQ, [(i - 1, i) for i in range(1, n)])


def ordered(first, own, other, axis):
    return jnp.where(
        first, jnp.concatenate([own, other], axis), jnp.concatenate([other, own], axis)
    )


def own_columns(weight, core, xp):
    mine = lax.dynamic_slice(weight, (0, core * 1024 + xp * 512), (28, 512))
    theirs = lax.dynamic_slice(weight, (0, (1 - core) * 1024 + xp * 512), (28, 512))
    return mine, theirs


def gather_z(block):
    copies = jnp.broadcast_to(block[None], (N_Z,) + block.shape)
    return lax.all_to_all(copies, "z", 0, 0)


def spread(part):
    lo, hi = part[:4], part[4:]
    return tuple((send(lo, -dx, -dy), send(hi, dx, dy)) for dx, dy in ((0, 1), (1, 0), (1, 1)))


def whole(part, arrived, ylo, xp):
    by_y, by_x, by_xy = (jnp.concatenate(pair, 0) for pair in arrived)
    same = ordered(xp == 0, part, by_x, 2)
    other = ordered(xp == 0, by_y, by_xy, 2)
    both = ordered(ylo == 0, same[:, None], other[:, None], 1)
    return both.reshape(896, 1024)


def dot(a, b, dims):
    return lax.dot_general(a, b, (dims, ((), ())), preferred_element_type=jnp.float32)


def key_kernel(enc_ref, weight_ref, query_ref, cot_ref, key_ref, prob_ref, term_ref, grad, total):
    step = pl.program_id(0)
    enc = enc_ref[0]
    key_ref[0] = dot(enc, weight_ref[...], ((1,), (0,))).astype(jnp.bfloat16)
    for head in range(8):
        cols = slice(head * HEAD_DIM, (head + 1) * HEAD_DIM)
        scores = dot(query_ref[0, :, cols], key_ref[0, :, cols], ((1,), (1,))) * SCALE
        weights = jnp.exp(scores - jnp.max(scores, axis=-1, keepdims=True))
        probs = weights / jnp.sum(weights, axis=-1, keepdims=True)
        prob_ref[0, head] = probs
        grad[:, cols] = dot(
            probs.astype(jnp.bfloat16), cot_ref[0, :, cols], ((0,), (0,))
        ).astype(jnp.bfloat16)
    term = dot(enc, grad[...], ((0,), (0,)))

    @pl.when(step == 0)
    def _():
        total[...] = term

    @pl.when(step > 0)
    def _():
        total[...] += term

    @pl.when(step == pl.num_programs(0) - 1)
    def _():
        term_ref[...] = total[...].astype(jnp.bfloat16)


def block_spec(*shape):
    return pl.BlockSpec((1,) + shape, lambda i: (i,) + (0,) * len(shape))


def full_spec(*shape):
    return pl.BlockSpec(shape, lambda i: (0,) * len(shape))


def key_part(enc, weight, query, cot):
    return pl.pallas_call(
        key_kernel,
        grid=(4,),
        in_specs=[
            block_spec(SPAN, 896),
            full_spec(896, 1024),
            block_spec(BLOCK, 1024),
            block_spec(BLOCK, 1024),
        ],
        out_specs=[
            block_spec(SPAN, 1024),
            block_spec(8, BLOCK, SPAN),
            full_spec(896, 1024),
        ],
        out_shape=[
            jax.ShapeDtypeStruct((4, SPAN, 1024), jnp.bfloat16),
            jax.ShapeDtypeStruct((4, 8, BLOCK, SPAN), jnp.float32),
            jax.ShapeDtypeStruct((896, 1024), jnp.bfloat16),
        ],
        scratch_shapes=[
            pltpu.VMEM((SPAN, 1024), jnp.bfloat16),
            pltpu.VMEM((896, 1024), jnp.float32),
        ],
        compiler_params=pltpu.CompilerParams(vmem_limit_bytes=VMEM),
        cost_estimate=pl.CostEstimate(
            flops=4_000_000_000, bytes_accessed=12_000_000, transcendentals=524288
        ),
        name="key_part",
    )(enc, weight, query, cot)


def value_kernel(enc_ref, weight_ref, key_ref, prob_ref, cot_ref, att_ref, qgrad_ref, value):
    value[...] = dot(enc_ref[0], weight_ref[...], ((1,), (0,))).astype(jnp.bfloat16)
    for head in range(8):
        cols = slice(head * HEAD_DIM, (head + 1) * HEAD_DIM)
        probs = prob_ref[0, head]
        cot = cot_ref[0, :, cols]
        attended = dot(probs.astype(jnp.bfloat16), value[:, cols], ((1,), (0,)))
        attended = attended.astype(jnp.bfloat16)
        prob_grad = dot(cot, value[:, cols], ((1,), (1,)))
        row_total = jnp.sum(
            cot.astype(jnp.float32) * attended.astype(jnp.float32), axis=-1, keepdims=True
        )
        score_grad = (SCALE * probs * (prob_grad - row_total)).astype(jnp.bfloat16)
        att_ref[0, :, cols] = attended
        qgrad_ref[0, :, cols] = dot(score_grad, key_ref[0, :, cols], ((1,), (0,))).astype(
            jnp.bfloat16
        )


def value_part(enc, weight, keys, probs, cot):
    return pl.pallas_call(
        value_kernel,
        grid=(4,),
        in_specs=[
            block_spec(SPAN, 896),
            full_spec(896, 1024),
            block_spec(SPAN, 1024),
            block_spec(8, BLOCK, SPAN),
            block_spec(BLOCK, 1024),
        ],
        out_specs=[block_spec(BLOCK, 1024), block_spec(BLOCK, 1024)],
        out_shape=[jax.ShapeDtypeStruct((4, BLOCK, 1024), jnp.bfloat16)] * 2,
        scratch_shapes=[pltpu.VMEM((SPAN, 1024), jnp.bfloat16)],
        compiler_params=pltpu.CompilerParams(vmem_limit_bytes=VMEM),
        cost_estimate=pl.CostEstimate(
            flops=2_500_000_000, bytes_accessed=10_000_000, transcendentals=0
        ),
        name="value_part",
    )(enc, weight, keys, probs, cot)


def quarter(term, ylo, xp):
    part = lax.dynamic_slice(term, (0, ylo, 0, xp * 512), (N_Z, 1, 56, 512))
    return part.reshape(N_Z, 56, 512)


def body(queries, pool, slots, key_weight, value_weight, cotangent):
    core, xp, ylo = lax.axis_index("core"), lax.axis_index("xp"), lax.axis_index("ylo")
    bf16, f32 = jnp.bfloat16, jnp.float32

    key_mine, key_theirs = own_columns(key_weight, core, xp)
    value_mine, value_theirs = own_columns(value_weight, core, xp)
    came = swap(jnp.concatenate([key_theirs, value_theirs], 1))
    key_block = ordered(core == 0, key_mine, came[:, :512], 0)
    value_block = ordered(core == 0, value_mine, came[:, 512:], 0)
    key_part_z = gather_z(key_block)
    key_spread = spread(key_part_z)

    rows = jnp.take(pool[0], slots[0].reshape(-1), axis=0).reshape(2, SPAN, 896)
    earlier = jnp.stack([next_group(rows[1]), rows[0]])
    enc = jnp.concatenate([earlier, swap(earlier)])

    def halves(x):
        x = x[0]
        mine = lax.dynamic_slice(x, (0, core * 1024), (128, 1024))
        theirs = lax.dynamic_slice(x, (0, (1 - core) * 1024), (128, 1024))
        return mine, theirs

    query_mine, query_theirs = halves(queries)
    cot_mine, cot_theirs = halves(cotangent)
    token_came = swap(jnp.stack([query_theirs, cot_theirs]))
    query = jnp.concatenate([query_mine, token_came[0]]).reshape(4, BLOCK, 1024)
    cot = jnp.concatenate([cot_mine, token_came[1]]).reshape(4, BLOCK, 1024)

    key_whole = whole(key_part_z, key_spread, ylo, xp)
    keys, probs, term = key_part(enc, key_whole, query, cot)

    term = term.reshape(N_Z, 2, 56, 1024)
    sums = quarter(term, ylo, xp).astype(f32)
    arrived = []
    for dx, dy in ((0, 1), (1, 0), (1, 1)):
        piece = quarter(term, ylo ^ dy, xp ^ dx)
        arrived.append((send(piece[:4], -dx, -dy), send(piece[4:], dx, dy)))

    value_part_z = gather_z(after(value_block, term))
    value_spread = spread(value_part_z)

    for pair in arrived:
        sums = sums + jnp.concatenate(pair, 0).astype(f32)
    along_z = lax.all_to_all(sums.astype(bf16), "z", 0, 0)
    sums = jnp.sum(along_z.astype(f32), axis=0)
    sums = sums.reshape(2, 2, 14, 4, 128).transpose(1, 3, 0, 2, 4)
    left = lax.all_to_all(sums.astype(bf16).reshape(8, 2, 14, 128), ("xh", "yhi"), 0, 0)
    done = jnp.sum(left.astype(f32), axis=0).astype(bf16)
    copies = jnp.broadcast_to(done[None], (16, 2, 14, 128)).reshape(32, 14, 128)
    pieces = lax.all_to_all(copies, ("yhi", "xh", "xp", "core"), 0, 0)
    pieces = pieces.reshape(4, 2, 2, 2, 14, 128).transpose(1, 4, 3, 2, 0, 5)
    weight_grad = pieces.reshape(28, 2048).astype(f32)

    value_whole = whole(value_part_z, value_spread, ylo, xp)
    att, qgrad = value_part(enc, value_whole, keys, probs, cot)
    att, qgrad = att.reshape(2, 128, 1024), qgrad.reshape(2, 128, 1024)
    out_came = swap(jnp.stack([att[1], qgrad[1]]))
    attended = ordered(core == 0, att[0], out_came[0], 1)
    query_grad = ordered(core == 0, qgrad[0], out_came[1], 1)
    return attended[None], query_grad[None], weight_grad


def solution(mesh):
    fine = Mesh(mesh.devices.reshape(SIZES), AXES)
    by_token = P(DP, SEQ, None)
    return jax.shard_map(
        body,
        mesh=fine,
        in_specs=(
            by_token,
            P(DP, SEQ, None, None),
            by_token,
            P(DP, None),
            P(DP, None),
            by_token,
        ),
        out_specs=(by_token, by_token, P(DP, None)),
        check_vma=False,
    )
```

time: 420 us -> 207 us (0.49)
  the two profiles are of different devices: /device:TPU:22 before, /device:TPU:1 now
where the time goes in v1:
time: 207 us; the launch traced here: 205 us
  starting transfers between devices  100 us (48%)
  blocking collectives  29 us (14%)
  waiting for transfers between devices  20.8 us (10%)
  Pallas kernels  20.1 us (10%)
  local copies, waits for them, and re-layouts  18.4 us (9%)
  other arithmetic  15.4 us (7%)
    ppermute x22, starting transfers between devices, send(): return lax.ppermute(value, AXES, route(dx, dy, flip))  78.4 us
    all_to_all x1, blocking collectives, body(): pieces = lax.all_to_all(copies, ('yhi', 'xh', 'xp', 'core'), 0, 0)  14.9 us
    all_to_all x1, blocking collectives, body(): lax.all_to_all(sums.astype(bf16).reshape(8, 2, 14, 128), ('xh', 'yhi'), 0...  14.1 us
    all_to_all x2, starting transfers between devices, gather_z(): return lax.all_to_all(copies, 'z', 0, 0)  14 us
    ppermute x22, waiting for transfers between devices, send(): return lax.ppermute(value, AXES, route(dx, dy, flip))  13.1 us
    pallas_call x1, Pallas kernels, key_part(): pl.pallas_call(key_kernel, grid=(4,), in_specs=[block_spec(SPAN, 896), fu...  10.5 us
    pallas_call x1, Pallas kernels, value_part(): pl.pallas_call(value_kernel, grid=(4,), in_specs=[block_spec(SPAN, 896),...  9.6 us
    all_to_all x2, waiting for transfers between devices, gather_z(): return lax.all_to_all(copies, 'z', 0, 0)  7.72 us
  transfers between devices with their start and end apart: 26, of which 4 were waited for; matrix products, arithmetic and copies ran while one was open for 12% of the time, Pallas kernels for 5%

profile of v1, /device:TPU:1, one launch (start us, length us, event | category | flops | bytes accessed | tf_op | source)
XLA Modules:
  0.0 205.3 jit_solution(3083220871953605305)
XLA Ops:
  0.7 1.5 constant_dynamic-slice_fusion.2
  2.2 8.8 %collective-permute-start.2 = (bf16[28,1024]{1,0:T(8,128)(2,1)S(1)}, bf16[28,1024]{1,0:T(8,128)(2,1)S(1)}, u32[]{:S(2)}, u32[]{:S(2)}) collective-permute-start(bf16[28,1024]{1,0:T(8,128)(2,1)S(1)} %pad_maximum_fusion.6), channel_id=1, source_target_pairs={{0,1},{1,0},{2,3},{3,2},{4,5},{5,4},{6,7},{7,6},{8,9},{9,8},{10,11... | collective-permute-start | bytes 172040 | tf_op jit(solution)/shard_map/ppermute | solution.py:40
  14.3 1.3 collective-permute-start
  15.6 2.0 dynamic-slice_bitcast_fusion.1
  19.0 6.5 %all-to-all-start = ((bf16[8,56,512]{2,1,0:T(8,128)(2,1)}), bf16[8,56,512]{2,1,0:T(8,128)(2,1)S(1)}, u32[]{:S(2)}, u32[]{:S(2)}) async-start(bf16[8,56,512]{2,1,0:T(8,128)(2,1)} %broadcast_in_dim.18), calls=%async_computation | async-start | bytes 917504 | tf_op jit(solution)/shard_map/all_to_all | solution.py:70
  26.4 2.5 %collective-permute-start.9 = (bf16[2,128,1024]{2,1,0:T(8,128)(2,1)}, bf16[2,128,1024]{2,1,0:T(8,128)(2,1)}, u32[]{:S(2)}, u32[]{:S(2)}) collective-permute-start(bf16[2,128,1024]{2,1,0:T(8,128)(2,1)} %pad_maximum_fusion.2), channel_id=1, source_target_pairs={{0,1},{1,0},{2,3},{3,2},{4,5},{5,4},{6,7},{7,6},{8,9},{9,8},{10,11... | collective-permute-start | bytes 1572872 | tf_op jit(solution)/shard_map/ppermute | solution.py:40
  28.9 1.5 maximum_select_fusion.6
  30.4 1.0 pad_maximum_fusion.1
  31.4 1.9 collective-permute-start.1
  33.3 1.1 slice_bitcast_fusion
  34.4 7.7 %all-to-all-done = bf16[8,56,512]{2,1,0:T(8,128)(2,1)S(1)} async-done(((bf16[8,56,512]{2,1,0:T(8,128)(2,1)}), bf16[8,56,512]{2,1,0:T(8,128)(2,1)S(1)}, u32[]{:S(2)}, u32[]{:S(2)}) %all-to-all-start) | async-done | bytes 458784 | tf_op jit(solution)/shard_map/all_to_all | solution.py:70
  42.1 5.1 %collective-permute-start.5 = (bf16[4,56,512]{2,1,0:T(8,128)(2,1)S(1)}, bf16[4,56,512]{2,1,0:T(8,128)(2,1)S(1)}, u32[]{:S(2)}, u32[]{:S(2)}) collective-permute-start(bf16[4,56,512]{2,1,0:T(8,128)(2,1)S(1)} %get-tuple-element.36), channel_id=1, source_target_pairs={{0,386},{1,387},{2,0},{3,1},{4,390},{5,391},{6,4},{7,5},{8,394},{9... | collective-permute-start | bytes 688136 | tf_op jit(solution)/shard_map/ppermute | solution.py:40
  47.2 1.9 collective-permute-start.6
  49.1 1.0 pad_maximum_fusion.4
  50.1 5.0 %collective-permute-start.7 = (bf16[4,56,512]{2,1,0:T(8,128)(2,1)S(1)}, bf16[4,56,512]{2,1,0:T(8,128)(2,1)S(1)}, u32[]{:S(2)}, u32[]{:S(2)}) collective-permute-start(bf16[4,56,512]{2,1,0:T(8,128)(2,1)S(1)} %get-tuple-element.36), channel_id=1, source_target_pairs={{0,482},{1,483},{2,96},{3,97},{4,486},{5,487},{6,100},{7,101},{8,4... | collective-permute-start | bytes 688136 | tf_op jit(solution)/shard_map/ppermute | solution.py:40
  55.2 1.9 collective-permute-start.8
  57.1 4.1 %collective-permute-start.3 = (bf16[4,56,512]{2,1,0:T(8,128)(2,1)S(1)}, bf16[4,56,512]{2,1,0:T(8,128)(2,1)S(1)}, u32[]{:S(2)}, u32[]{:S(2)}) collective-permute-start(bf16[4,56,512]{2,1,0:T(8,128)(2,1)S(1)} %get-tuple-element.36), channel_id=1, source_target_pairs={{0,96},{1,97},{2,98},{3,99},{4,100},{5,101},{6,102},{7,103},{8,104... | collective-permute-start | bytes 688136 | tf_op jit(solution)/shard_map/ppermute | solution.py:40
  61.3 1.9 collective-permute-start.4
  63.3 2.9 %collective-permute-done.8 = bf16[4,56,512]{2,1,0:T(8,128)(2,1)S(1)} collective-permute-done((bf16[4,56,512]{2,1,0:T(8,128)(2,1)S(1)}, bf16[4,56,512]{2,1,0:T(8,128)(2,1)S(1)}, u32[]{:S(2)}, u32[]{:S(2)}) %collective-permute-start.8) | collective-permute-done | bytes 229408 | tf_op jit(solution)/shard_map/ppermute | solution.py:40
  66.2 5.2 %collective-permute-done.4 = bf16[4,56,512]{2,1,0:T(8,128)(2,1)S(1)} collective-permute-done((bf16[4,56,512]{2,1,0:T(8,128)(2,1)S(1)}, bf16[4,56,512]{2,1,0:T(8,128)(2,1)S(1)}, u32[]{:S(2)}, u32[]{:S(2)}) %collective-permute-start.4) | collective-permute-done | bytes 229408 | tf_op jit(solution)/shard_map/ppermute | solution.py:40
  72.2 1.4 pad_maximum_fusion.enc_ref
  73.6 10.5 %key_part.1 = (bf16[4,256,1024]{2,1,0:T(8,128)(2,1)S(1)}, f32[4,8,64,256]{3,2,1,0:T(8,128)}, bf16[896,1024]{1,0:T(8,128)(2,1)S(1)}) custom-call(bf16[4,256,896]{2,1,0:T(8,128)(2,1)S(1)} %pad_maximum_fusion.enc_ref, bf16[896,1024]{1,0:T(8,128)(2,1)S(1)} %bitcast.94, bf16[4,64,1024]{2,1,0:T(8,128)(2,1)S(1)} %bitcast.98, bf16[4,64,1024]{2,1,0:T(8,128)(2,1)S(1)} %bitcast.96), custom_call_target="tpu_custom_call" | custom-call | flops 4000000000 | bytes 12000000 | tf_op jit(solution)/shard_map/key_part/pallas_call | solution.py:127
  84.1 1.3 copy-done.5
  86.2 7.5 %all-to-all-start.1 = ((bf16[8,56,512]{2,1,0:T(8,128)(2,1)}), bf16[8,56,512]{2,1,0:T(8,128)(2,1)}, u32[]{:S(2)}, u32[]{:S(2)}) async-start(bf16[8,56,512]{2,1,0:T(8,128)(2,1)} %broadcast_in_dim.19), calls=%async_computation.1 | async-start | bytes 917504 | tf_op jit(solution)/shard_map/all_to_all | solution.py:70
  94.7 3.0 %collective-permute-start.17 = (bf16[4,56,512]{2,1,0:T(8,128)(2,1)S(1)}, bf16[4,56,512]{2,1,0:T(8,128)(2,1)S(1)}, u32[]{:S(2)}, u32[]{:S(2)}) collective-permute-start(bf16[4,56,512]{2,1,0:T(8,128)(2,1)S(1)} %get-tuple-element.17), channel_id=1, source_target_pairs={{0,386},{1,387},{2,0},{3,1},{4,390},{5,391},{6,4},{7,5},{8,394},{9... | collective-permute-start | bytes 688136 | tf_op jit(solution)/shard_map/ppermute | solution.py:40
  97.7 2.2 %collective-permute-start.18 = (bf16[4,56,512]{2,1,0:T(8,128)(2,1)}, bf16[4,56,512]{2,1,0:T(8,128)(2,1)}, u32[]{:S(2)}, u32[]{:S(2)}) collective-permute-start(bf16[4,56,512]{2,1,0:T(8,128)(2,1)} %get-tuple-element.18), channel_id=1, source_target_pairs={{0,2},{1,3},{2,128},{3,129},{4,6},{5,7},{6,132},{7,133},{8,10},{9,... | collective-permute-start | bytes 688136 | tf_op jit(solution)/shard_map/ppermute | solution.py:40
  100.0 1.9 collective-permute-start.19
  101.9 4.1 %collective-permute-start.20 = (bf16[4,56,512]{2,1,0:T(8,128)(2,1)}, bf16[4,56,512]{2,1,0:T(8,128)(2,1)}, u32[]{:S(2)}, u32[]{:S(2)}) collective-permute-start(bf16[4,56,512]{2,1,0:T(8,128)(2,1)} %get-tuple-element.19), channel_id=1, source_target_pairs={{0,32},{1,33},{2,34},{3,35},{4,36},{5,37},{6,38},{7,39},{8,40},{9,... | collective-permute-start | bytes 688136 | tf_op jit(solution)/shard_map/ppermute | solution.py:40
  106.0 3.1 %collective-permute-start.22 = (bf16[4,56,512]{2,1,0:T(8,128)(2,1)S(1)}, bf16[4,56,512]{2,1,0:T(8,128)(2,1)}, u32[]{:S(2)}, u32[]{:S(2)}) collective-permute-start(bf16[4,56,512]{2,1,0:T(8,128)(2,1)S(1)} %get-tuple-element.15), channel_id=1, source_target_pairs={{0,34},{1,35},{2,160},{3,161},{4,38},{5,39},{6,164},{7,165},{8,42}... | collective-permute-start | bytes 688136 | tf_op jit(solution)/shard_map/ppermute | solution.py:40
  110.5 5.5 %collective-permute-start.21 = (bf16[4,56,512]{2,1,0:T(8,128)(2,1)}, bf16[4,56,512]{2,1,0:T(8,128)(2,1)}, u32[]{:S(2)}, u32[]{:S(2)}) collective-permute-start(bf16[4,56,512]{2,1,0:T(8,128)(2,1)} %slice_bitcast_fusion.2), channel_id=1, source_target_pairs={{0,482},{1,483},{2,96},{3,97},{4,486},{5,487},{6,100},{7,101},{8,4... | collective-permute-start | bytes 688136 | tf_op jit(solution)/shard_map/ppermute | solution.py:40
  116.1 1.9 fusion.10
  117.9 1.9 collective-permute-start.10
  119.9 3.4 %collective-permute-start.11 = (bf16[4,56,512]{2,1,0:T(8,128)(2,1)}, bf16[4,56,512]{2,1,0:T(8,128)(2,1)}, u32[]{:S(2)}, u32[]{:S(2)}) collective-permute-start(bf16[4,56,512]{2,1,0:T(8,128)(2,1)} %get-tuple-element.35), channel_id=1, source_target_pairs={{0,32},{1,33},{2,34},{3,35},{4,36},{5,37},{6,38},{7,39},{8,40},{9,... | collective-permute-start | bytes 688136 | tf_op jit(solution)/shard_map/ppermute | solution.py:40
  123.2 2.3 %collective-permute-start.12 = (bf16[4,56,512]{2,1,0:T(8,128)(2,1)}, bf16[4,56,512]{2,1,0:T(8,128)(2,1)}, u32[]{:S(2)}, u32[]{:S(2)}) collective-permute-start(bf16[4,56,512]{2,1,0:T(8,128)(2,1)} %get-tuple-element.34), channel_id=1, source_target_pairs={{0,386},{1,387},{2,0},{3,1},{4,390},{5,391},{6,4},{7,5},{8,394},{9... | collective-permute-start | bytes 688136 | tf_op jit(solution)/shard_map/ppermute | solution.py:40
  125.5 3.0 %collective-permute-start.13 = (bf16[4,56,512]{2,1,0:T(8,128)(2,1)}, bf16[4,56,512]{2,1,0:T(8,128)(2,1)S(1)}, u32[]{:S(2)}, u32[]{:S(2)}) collective-permute-start(bf16[4,56,512]{2,1,0:T(8,128)(2,1)} %get-tuple-element.35), channel_id=1, source_target_pairs={{0,2},{1,3},{2,128},{3,129},{4,6},{5,7},{6,132},{7,133},{8,10},{9,... | collective-permute-start | bytes 688136 | tf_op jit(solution)/shard_map/ppermute | solution.py:40
  128.6 2.5 %fusion.4 = bf16[8,56,512]{2,1,0:T(8,128)(2,1)} fusion(bf16[4,56,512]{2,1,0:T(8,128)(2,1)} %collective-permute-done.18, bf16[4,56,512]{2,1,0:T(8,128)(2,1)} %copy-done.9, bf16[4,56,512]{2,1,0:T(8,128)(2,1)} %collective-permute-done.20, bf16[4,56,512]{2,1,0:T(8,128)(2,1)} %collective-permute-done.19, bf16[4,56,512]{2,1,0:T(8,128)(2,1)} %collective-permute-done.22, ...), kind=kLoop, calls=%fused_computation.16 | loop fusion | flops 3899392 | bytes 2293768 | tf_op jit(solution)/shard_map/convert_element_type | solution.py:247
  131.0 6.6 %all-to-all-start.2 = ((bf16[8,56,512]{2,1,0:T(8,128)(2,1)}), bf16[8,56,512]{2,1,0:T(8,128)(2,1)S(1)}, u32[]{:S(2)}, u32[]{:S(2)}) async-start(bf16[8,56,512]{2,1,0:T(8,128)(2,1)} %fusion.4), calls=%async_computation.2 | async-start | bytes 917504 | tf_op jit(solution)/shard_map/all_to_all | solution.py:247
  137.7 4.4 %collective-permute-start.14 = (bf16[4,56,512]{2,1,0:T(8,128)(2,1)}, bf16[4,56,512]{2,1,0:T(8,128)(2,1)S(1)}, u32[]{:S(2)}, u32[]{:S(2)}) collective-permute-start(bf16[4,56,512]{2,1,0:T(8,128)(2,1)} %get-tuple-element.34), channel_id=1, source_target_pairs={{0,482},{1,483},{2,96},{3,97},{4,486},{5,487},{6,100},{7,101},{8,4... | collective-permute-start | bytes 688136 | tf_op jit(solution)/shard_map/ppermute | solution.py:40
  142.1 1.9 collective-permute-start.15
  144.1 1.1 maximum_bitcast_fusion.7
  145.2 1.0 maximum_bitcast_fusion.8
  146.2 1.6 fusion.1
  147.8 4.9 %collective-permute-done.15 = bf16[4,56,512]{2,1,0:T(8,128)(2,1)S(1)} collective-permute-done((bf16[4,56,512]{2,1,0:T(8,128)(2,1)}, bf16[4,56,512]{2,1,0:T(8,128)(2,1)S(1)}, u32[]{:S(2)}, u32[]{:S(2)}) %collective-permute-start.15) | collective-permute-done | bytes 229408 | tf_op jit(solution)/shard_map/ppermute | solution.py:40
  153.2 1.1 copy-done.6
  155.0 9.6 %value_part.1 = (bf16[4,64,1024]{2,1,0:T(8,128)(2,1)S(1)}, bf16[4,64,1024]{2,1,0:T(8,128)(2,1)S(1)}) custom-call(bf16[4,256,896]{2,1,0:T(8,128)(2,1)S(1)} %copy-done.2, bf16[896,1024]{1,0:T(8,128)(2,1)S(1)} %bitcast.95, bf16[4,256,1024]{2,1,0:T(8,128)(2,1)S(1)} %copy-done.6, f32[4,8,64,256]{3,2,1,0:T(8,128)S(1)} %copy-done.7, bf16[4,64,1024]{2,1,0:T(8,128)(2,1)S(1)} %bitcast.97), custom_call_target="tpu_custom_call" | custom-call | flops 2500000000 | bytes 10000000 | tf_op jit(solution)/shard_map/value_part/pallas_call | solution.py:178
  164.8 8.5 %collective-permute-start.16 = (bf16[2,128,1024]{2,1,0:T(8,128)(2,1)S(1)}, bf16[2,128,1024]{2,1,0:T(8,128)(2,1)S(1)}, u32[]{:S(2)}, u32[]{:S(2)}) collective-permute-start(bf16[2,128,1024]{2,1,0:T(8,128)(2,1)S(1)} %pad_maximum_fusion.5), channel_id=1, source_target_pairs={{0,1},{1,0},{2,3},{3,2},{4,5},{5,4},{6,7},{7,6},{8,9},{9,8},{10,11... | collective-permute-start | bytes 1572872 | tf_op jit(solution)/shard_map/ppermute | solution.py:40
  173.5 14.1 %all_to_all.25 = bf16[8,2,14,128]{3,1,2,0:T(2,128)(2,1)S(1)} all-to-all(bf16[8,2,14,128]{3,1,2,0:T(2,128)(2,1)S(1)} %copy.70), channel_id=1, replica_groups=mesh['yhi'=4,'xh'=2,'xp'=2,'z'=8,'ylo'=2,'core'=2] {'xh','yhi'}, dimensions={0} | all-to-all | bytes 114688 | tf_op jit(solution)/shard_map/all_to_all | solution.py:250
  187.7 14.9 %all_to_all.26 = bf16[32,14,128]{2,1,0:T(8,128)(2,1)S(1)} all-to-all(bf16[32,14,128]{2,1,0:T(8,128)(2,1)S(1)} %bitcast.109), channel_id=1, replica_groups=mesh['yhi'=4,'xh'=2,'xp'=2,'z'=8,'ylo'=2,'core'=2] {'yhi','xh','xp','core'}, dimensions={0} | all-to-all | bytes 229376 | tf_op jit(solution)/shard_map/all_to_all | solution.py:253
  (84 shorter events, 14.0 us)
Async XLA Ops:
  0.6 11.9 %copy-start = (bf16[1,6,128,896]{3,2,1,0:T(8,128)(2,1)S(1)}, bf16[1,6,128,896]{3,2,1,0:T(8,128)(2,1)}, u32[]{:S(2)}) copy-start(bf16[1,6,128,896]{3,2,1,0:T(8,128)(2,1)} %param.7) | copy-start | bytes 4128772
  2.2 15.4 %collective-permute-start.2 = (bf16[28,1024]{1,0:T(8,128)(2,1)S(1)}, bf16[28,1024]{1,0:T(8,128)(2,1)S(1)}, u32[]{:S(2)}, u32[]{:S(2)}) collective-permute-start(bf16[28,1024]{1,0:T(8,128)(2,1)S(1)} %pad_maximum_fusion.6), channel_id=1, source_target_pairs={{0,1},{1,0},{2,3},{3,2},{4,5},{5,4},{6,7},{7,6},{8,9},{9,8},{10,11... | collective-permute-start | bytes 172040 | tf_op jit(solution)/shard_map/ppermute | solution.py:40
  14.3 16.1 %collective-permute-start = (bf16[256,896]{1,0:T(8,128)(2,1)}, bf16[256,896]{1,0:T(8,128)(2,1)S(1)}, u32[]{:S(2)}, u32[]{:S(2)}) collective-permute-start(bf16[256,896]{1,0:T(8,128)(2,1)} %bitcast.2), channel_id=1, source_target_pairs={{0,32},{32,64},{64,96},{96,128},{128,160},{160,192},{192,224},{224... | collective-permute-start | bytes 1376264 | tf_op jit(solution)/shard_map/ppermute | solution.py:53
  19.0 23.0 %all-to-all-start = ((bf16[8,56,512]{2,1,0:T(8,128)(2,1)}), bf16[8,56,512]{2,1,0:T(8,128)(2,1)S(1)}, u32[]{:S(2)}, u32[]{:S(2)}) async-start(bf16[8,56,512]{2,1,0:T(8,128)(2,1)} %broadcast_in_dim.18), calls=%async_computation | async-start | bytes 917504 | tf_op jit(solution)/shard_map/all_to_all | solution.py:70
  26.4 6.9 %collective-permute-start.9 = (bf16[2,128,1024]{2,1,0:T(8,128)(2,1)}, bf16[2,128,1024]{2,1,0:T(8,128)(2,1)}, u32[]{:S(2)}, u32[]{:S(2)}) collective-permute-start(bf16[2,128,1024]{2,1,0:T(8,128)(2,1)} %pad_maximum_fusion.2), channel_id=1, source_target_pairs={{0,1},{1,0},{2,3},{3,2},{4,5},{5,4},{6,7},{7,6},{8,9},{9,8},{10,11... | collective-permute-start | bytes 1572872 | tf_op jit(solution)/shard_map/ppermute | solution.py:40
  31.4 40.8 %collective-permute-start.1 = (bf16[2,256,896]{2,1,0:T(8,128)(2,1)}, bf16[2,256,896]{2,1,0:T(8,128)(2,1)}, u32[]{:S(2)}, u32[]{:S(2)}) collective-permute-start(bf16[2,256,896]{2,1,0:T(8,128)(2,1)} %pad_maximum_fusion.1), channel_id=1, source_target_pairs={{0,1},{1,0},{2,3},{3,2},{4,5},{5,4},{6,7},{7,6},{8,9},{9,8},{10,11... | collective-permute-start | bytes 2752520 | tf_op jit(solution)/shard_map/ppermute | solution.py:40
  42.1 15.0 %collective-permute-start.5 = (bf16[4,56,512]{2,1,0:T(8,128)(2,1)S(1)}, bf16[4,56,512]{2,1,0:T(8,128)(2,1)S(1)}, u32[]{:S(2)}, u32[]{:S(2)}) collective-permute-start(bf16[4,56,512]{2,1,0:T(8,128)(2,1)S(1)} %get-tuple-element.36), channel_id=1, source_target_pairs={{0,386},{1,387},{2,0},{3,1},{4,390},{5,391},{6,4},{7,5},{8,394},{9... | collective-permute-start | bytes 688136 | tf_op jit(solution)/shard_map/ppermute | solution.py:40
  47.2 14.1 %collective-permute-start.6 = (bf16[4,56,512]{2,1,0:T(8,128)(2,1)S(1)}, bf16[4,56,512]{2,1,0:T(8,128)(2,1)S(1)}, u32[]{:S(2)}, u32[]{:S(2)}) collective-permute-start(bf16[4,56,512]{2,1,0:T(8,128)(2,1)S(1)} %get-tuple-element.37), channel_id=1, source_target_pairs={{0,2},{1,3},{2,128},{3,129},{4,6},{5,7},{6,132},{7,133},{8,10},{9,... | collective-permute-start | bytes 688136 | tf_op jit(solution)/shard_map/ppermute | solution.py:40
  50.1 23.5 %copy-start.3 = (bf16[256,1024]{1,0:T(8,128)(2,1)}, bf16[256,1024]{1,0:T(8,128)(2,1)S(1)}, u32[]{:S(2)}) copy-start(bf16[256,1024]{1,0:T(8,128)(2,1)S(1)} %pad_maximum_fusion.4) | copy-start | bytes 1572868
  50.1 13.1 %collective-permute-start.7 = (bf16[4,56,512]{2,1,0:T(8,128)(2,1)S(1)}, bf16[4,56,512]{2,1,0:T(8,128)(2,1)S(1)}, u32[]{:S(2)}, u32[]{:S(2)}) collective-permute-start(bf16[4,56,512]{2,1,0:T(8,128)(2,1)S(1)} %get-tuple-element.36), channel_id=1, source_target_pairs={{0,482},{1,483},{2,96},{3,97},{4,486},{5,487},{6,100},{7,101},{8,4... | collective-permute-start | bytes 688136 | tf_op jit(solution)/shard_map/ppermute | solution.py:40
  55.2 11.0 %collective-permute-start.8 = (bf16[4,56,512]{2,1,0:T(8,128)(2,1)S(1)}, bf16[4,56,512]{2,1,0:T(8,128)(2,1)S(1)}, u32[]{:S(2)}, u32[]{:S(2)}) collective-permute-start(bf16[4,56,512]{2,1,0:T(8,128)(2,1)S(1)} %get-tuple-element.37), channel_id=1, source_target_pairs={{0,34},{1,35},{2,160},{3,161},{4,38},{5,39},{6,164},{7,165},{8,42}... | collective-permute-start | bytes 688136 | tf_op jit(solution)/shard_map/ppermute | solution.py:40
  57.1 9.1 %collective-permute-start.3 = (bf16[4,56,512]{2,1,0:T(8,128)(2,1)S(1)}, bf16[4,56,512]{2,1,0:T(8,128)(2,1)S(1)}, u32[]{:S(2)}, u32[]{:S(2)}) collective-permute-start(bf16[4,56,512]{2,1,0:T(8,128)(2,1)S(1)} %get-tuple-element.36), channel_id=1, source_target_pairs={{0,96},{1,97},{2,98},{3,99},{4,100},{5,101},{6,102},{7,103},{8,104... | collective-permute-start | bytes 688136 | tf_op jit(solution)/shard_map/ppermute | solution.py:40
  61.3 10.1 %collective-permute-start.4 = (bf16[4,56,512]{2,1,0:T(8,128)(2,1)S(1)}, bf16[4,56,512]{2,1,0:T(8,128)(2,1)S(1)}, u32[]{:S(2)}, u32[]{:S(2)}) collective-permute-start(bf16[4,56,512]{2,1,0:T(8,128)(2,1)S(1)} %get-tuple-element.37), channel_id=1, source_target_pairs={{0,32},{1,33},{2,34},{3,35},{4,36},{5,37},{6,38},{7,39},{8,40},{9,... | collective-permute-start | bytes 688136 | tf_op jit(solution)/shard_map/ppermute | solution.py:40
  73.6 10.5 %copy-start.1 = (bf16[4,256,896]{2,1,0:T(8,128)(2,1)}, bf16[4,256,896]{2,1,0:T(8,128)(2,1)S(1)}, u32[]{:S(2)}) copy-start(bf16[4,256,896]{2,1,0:T(8,128)(2,1)S(1)} %pad_maximum_fusion.enc_ref) | copy-start | bytes 5505028
  73.6 11.8 %copy-start.8 = (bf16[56,512]{1,0:T(8,128)(2,1)S(1)}, bf16[56,512]{1,0:T(8,128)(2,1)}, u32[]{:S(2)}) copy-start(bf16[56,512]{1,0:T(8,128)(2,1)} %maximum_select_fusion.6) | copy-start | bytes 172036
  84.1 1.3 copy-start.5
  86.2 29.9 %all-to-all-start.1 = ((bf16[8,56,512]{2,1,0:T(8,128)(2,1)}), bf16[8,56,512]{2,1,0:T(8,128)(2,1)}, u32[]{:S(2)}, u32[]{:S(2)}) async-start(bf16[8,56,512]{2,1,0:T(8,128)(2,1)} %broadcast_in_dim.19), calls=%async_computation.1 | async-start | bytes 917504 | tf_op jit(solution)/shard_map/all_to_all | solution.py:70
  94.7 15.2 %collective-permute-start.17 = (bf16[4,56,512]{2,1,0:T(8,128)(2,1)S(1)}, bf16[4,56,512]{2,1,0:T(8,128)(2,1)S(1)}, u32[]{:S(2)}, u32[]{:S(2)}) collective-permute-start(bf16[4,56,512]{2,1,0:T(8,128)(2,1)S(1)} %get-tuple-element.17), channel_id=1, source_target_pairs={{0,386},{1,387},{2,0},{3,1},{4,390},{5,391},{6,4},{7,5},{8,394},{9... | collective-permute-start | bytes 688136 | tf_op jit(solution)/shard_map/ppermute | solution.py:40
  97.7 20.2 %collective-permute-start.18 = (bf16[4,56,512]{2,1,0:T(8,128)(2,1)}, bf16[4,56,512]{2,1,0:T(8,128)(2,1)}, u32[]{:S(2)}, u32[]{:S(2)}) collective-permute-start(bf16[4,56,512]{2,1,0:T(8,128)(2,1)} %get-tuple-element.18), channel_id=1, source_target_pairs={{0,2},{1,3},{2,128},{3,129},{4,6},{5,7},{6,132},{7,133},{8,10},{9,... | collective-permute-start | bytes 688136 | tf_op jit(solution)/shard_map/ppermute | solution.py:40
  100.0 19.9 %collective-permute-start.19 = (bf16[4,56,512]{2,1,0:T(8,128)(2,1)}, bf16[4,56,512]{2,1,0:T(8,128)(2,1)}, u32[]{:S(2)}, u32[]{:S(2)}) collective-permute-start(bf16[4,56,512]{2,1,0:T(8,128)(2,1)} %get-tuple-element.16), channel_id=1, source_target_pairs={{0,96},{1,97},{2,98},{3,99},{4,100},{5,101},{6,102},{7,103},{8,104... | collective-permute-start | bytes 688136 | tf_op jit(solution)/shard_map/ppermute | solution.py:40
  101.9 21.3 %collective-permute-start.20 = (bf16[4,56,512]{2,1,0:T(8,128)(2,1)}, bf16[4,56,512]{2,1,0:T(8,128)(2,1)}, u32[]{:S(2)}, u32[]{:S(2)}) collective-permute-start(bf16[4,56,512]{2,1,0:T(8,128)(2,1)} %get-tuple-element.19), channel_id=1, source_target_pairs={{0,32},{1,33},{2,34},{3,35},{4,36},{5,37},{6,38},{7,39},{8,40},{9,... | collective-permute-start | bytes 688136 | tf_op jit(solution)/shard_map/ppermute | solution.py:40
  106.0 19.5 %collective-permute-start.22 = (bf16[4,56,512]{2,1,0:T(8,128)(2,1)S(1)}, bf16[4,56,512]{2,1,0:T(8,128)(2,1)}, u32[]{:S(2)}, u32[]{:S(2)}) collective-permute-start(bf16[4,56,512]{2,1,0:T(8,128)(2,1)S(1)} %get-tuple-element.15), channel_id=1, source_target_pairs={{0,34},{1,35},{2,160},{3,161},{4,38},{5,39},{6,164},{7,165},{8,42}... | collective-permute-start | bytes 688136 | tf_op jit(solution)/shard_map/ppermute | solution.py:40
  109.9 0.7 copy-start.9
  110.5 18.0 %collective-permute-start.21 = (bf16[4,56,512]{2,1,0:T(8,128)(2,1)}, bf16[4,56,512]{2,1,0:T(8,128)(2,1)}, u32[]{:S(2)}, u32[]{:S(2)}) collective-permute-start(bf16[4,56,512]{2,1,0:T(8,128)(2,1)} %slice_bitcast_fusion.2), channel_id=1, source_target_pairs={{0,482},{1,483},{2,96},{3,97},{4,486},{5,487},{6,100},{7,101},{8,4... | collective-permute-start | bytes 688136 | tf_op jit(solution)/shard_map/ppermute | solution.py:40
  117.9 24.2 %collective-permute-start.10 = (bf16[4,56,512]{2,1,0:T(8,128)(2,1)}, bf16[4,56,512]{2,1,0:T(8,128)(2,1)}, u32[]{:S(2)}, u32[]{:S(2)}) collective-permute-start(bf16[4,56,512]{2,1,0:T(8,128)(2,1)} %get-tuple-element.34), channel_id=1, source_target_pairs={{0,96},{1,97},{2,98},{3,99},{4,100},{5,101},{6,102},{7,103},{8,104... | collective-permute-start | bytes 688136 | tf_op jit(solution)/shard_map/ppermute | solution.py:40
  119.9 24.2 %collective-permute-start.11 = (bf16[4,56,512]{2,1,0:T(8,128)(2,1)}, bf16[4,56,512]{2,1,0:T(8,128)(2,1)}, u32[]{:S(2)}, u32[]{:S(2)}) collective-permute-start(bf16[4,56,512]{2,1,0:T(8,128)(2,1)} %get-tuple-element.35), channel_id=1, source_target_pairs={{0,32},{1,33},{2,34},{3,35},{4,36},{5,37},{6,38},{7,39},{8,40},{9,... | collective-permute-start | bytes 688136 | tf_op jit(solution)/shard_map/ppermute | solution.py:40
  123.2 21.9 %collective-permute-start.12 = (bf16[4,56,512]{2,1,0:T(8,128)(2,1)}, bf16[4,56,512]{2,1,0:T(8,128)(2,1)}, u32[]{:S(2)}, u32[]{:S(2)}) collective-permute-start(bf16[4,56,512]{2,1,0:T(8,128)(2,1)} %get-tuple-element.34), channel_id=1, source_target_pairs={{0,386},{1,387},{2,0},{3,1},{4,390},{5,391},{6,4},{7,5},{8,394},{9... | collective-permute-start | bytes 688136 | tf_op jit(solution)/shard_map/ppermute | solution.py:40
  125.5 19.6 %collective-permute-start.13 = (bf16[4,56,512]{2,1,0:T(8,128)(2,1)}, bf16[4,56,512]{2,1,0:T(8,128)(2,1)S(1)}, u32[]{:S(2)}, u32[]{:S(2)}) collective-permute-start(bf16[4,56,512]{2,1,0:T(8,128)(2,1)} %get-tuple-element.35), channel_id=1, source_target_pairs={{0,2},{1,3},{2,128},{3,129},{4,6},{5,7},{6,132},{7,133},{8,10},{9,... | collective-permute-start | bytes 688136 | tf_op jit(solution)/shard_map/ppermute | solution.py:40
  131.0 42.2 %all-to-all-start.2 = ((bf16[8,56,512]{2,1,0:T(8,128)(2,1)}), bf16[8,56,512]{2,1,0:T(8,128)(2,1)S(1)}, u32[]{:S(2)}, u32[]{:S(2)}) async-start(bf16[8,56,512]{2,1,0:T(8,128)(2,1)} %fusion.4), calls=%async_computation.2 | async-start | bytes 917504 | tf_op jit(solution)/shard_map/all_to_all | solution.py:247
  137.7 10.1 %collective-permute-start.14 = (bf16[4,56,512]{2,1,0:T(8,128)(2,1)}, bf16[4,56,512]{2,1,0:T(8,128)(2,1)S(1)}, u32[]{:S(2)}, u32[]{:S(2)}) collective-permute-start(bf16[4,56,512]{2,1,0:T(8,128)(2,1)} %get-tuple-element.34), channel_id=1, source_target_pairs={{0,482},{1,483},{2,96},{3,97},{4,486},{5,487},{6,100},{7,101},{8,4... | collective-permute-start | bytes 688136 | tf_op jit(solution)/shard_map/ppermute | solution.py:40
  142.1 10.6 %collective-permute-start.15 = (bf16[4,56,512]{2,1,0:T(8,128)(2,1)}, bf16[4,56,512]{2,1,0:T(8,128)(2,1)S(1)}, u32[]{:S(2)}, u32[]{:S(2)}) collective-permute-start(bf16[4,56,512]{2,1,0:T(8,128)(2,1)} %get-tuple-element.35), channel_id=1, source_target_pairs={{0,34},{1,35},{2,160},{3,161},{4,38},{5,39},{6,164},{7,165},{8,42}... | collective-permute-start | bytes 688136 | tf_op jit(solution)/shard_map/ppermute | solution.py:40
  146.2 7.1 %copy-start.7 = (f32[4,8,64,256]{3,2,1,0:T(8,128)S(1)}, f32[4,8,64,256]{3,2,1,0:T(8,128)}, u32[]{:S(2)}) copy-start(f32[4,8,64,256]{3,2,1,0:T(8,128)} %get-tuple-element.12.prob_ref) | copy-start | bytes 6291460
  152.8 1.6 copy-start.6
  153.0 1.9 copy-start.2
  153.0 2.0 copy-start.4
  164.8 38.7 %collective-permute-start.16 = (bf16[2,128,1024]{2,1,0:T(8,128)(2,1)S(1)}, bf16[2,128,1024]{2,1,0:T(8,128)(2,1)S(1)}, u32[]{:S(2)}, u32[]{:S(2)}) collective-permute-start(bf16[2,128,1024]{2,1,0:T(8,128)(2,1)S(1)} %pad_maximum_fusion.5), channel_id=1, source_target_pairs={{0,1},{1,0},{2,3},{3,2},{4,5},{5,4},{6,7},{7,6},{8,9},{9,8},{10,11... | collective-permute-start | bytes 1572872 | tf_op jit(solution)/shard_map/ppermute | solution.py:40

commit v2 on v0

v2 whole, which is shorter than its diff:
```python
import math

import jax
import jax.numpy as jnp
from jax import lax
from jax.experimental import pallas as pl
from jax.experimental.pallas import tpu as pltpu
from jax.sharding import Mesh
from jax.sharding import PartitionSpec as P

HEAD_DIM = 128
BLOCK = 64
SPAN = 256
SCALE = 1.0 / math.sqrt(HEAD_DIM)

AXES = ("yhi", "xh", "xp", "zh", "zl", "ylo", "core")
SIZES = (4, 2, 2, 4, 2, 2, 2)
SEQ = ("yhi", "xh", "xp")
DP = ("zh", "zl", "ylo", "core")
CUBE = ("zl", "ylo", "xp")
VMEM = 60 * 1024 * 1024


def place(x, y, z, core):
    return (((y // 2 * 4 + x) * 8 + z) * 2 + y % 2) * 2 + core


def odd_square(dx, dy):
    return [
        (
            place(x, y, z, core),
            place((x + dx * (2 * (x % 2) - 1)) % 4, (y + dy * (2 * (y % 2) - 1)) % 8, z, core),
        )
        for x in range(4)
        for y in range(8)
        for z in range(8)
        for core in range(2)
    ]


ODD_SQUARE = [odd_square(1, 0), odd_square(0, 1), odd_square(1, 1)]
ODD_Z = [
    (place(x, y, z, core), place(x, y, (z + 2 * (z % 2) - 1) % 8, core))
    for x in range(4)
    for y in range(8)
    for z in range(8)
    for core in range(2)
]


def after(value, token):
    return lax.optimization_barrier((value, token))[0]


def swap(value):
    return lax.ppermute(value, "core", [(0, 1), (1, 0)])


def next_group(rows):
    n = 16
    return lax.ppermute(rows, SEQ, [(i - 1, i) for i in range(1, n)])


def ordered(first, own, other, axis):
    return jnp.where(
        first, jnp.concatenate([own, other], axis), jnp.concatenate([other, own], axis)
    )


def copies(value, count):
    return jnp.broadcast_to(value[None], (count,) + value.shape)


def dot(a, b, dims):
    return lax.dot_general(a, b, (dims, ((), ())), preferred_element_type=jnp.float32)


def pick(own, other):
    return jnp.where(pl.program_id(0) < 2, own, other)


def key_kernel(
    core_ref, own_ref, other_ref, weight_ref, query_ref, cot_ref, came_ref,
    key_ref, prob_ref, term_ref, total,
):
    step = pl.program_id(0)
    enc = pick(own_ref[0], other_ref[0])
    query = pick(query_ref[0], came_ref[0, 0])
    cot = pick(cot_ref[0], came_ref[1, 0])
    keys = dot(enc, weight_ref[...], ((1,), (0,))).astype(jnp.bfloat16)
    key_ref[0] = keys
    heads = [slice(h * HEAD_DIM, (h + 1) * HEAD_DIM) for h in range(8)]
    scores = [dot(query[:, cols], keys[:, cols], ((1,), (1,))) for cols in heads]
    scores = jnp.concatenate(scores) * SCALE
    weights = jnp.exp(scores - jnp.max(scores, axis=-1, keepdims=True))
    probs = weights * (1.0 / jnp.sum(weights, axis=-1, keepdims=True))
    prob_ref[0] = probs
    low = probs.astype(jnp.bfloat16)
    grads = [
        dot(low[h * BLOCK : (h + 1) * BLOCK], cot[:, cols], ((0,), (0,)))
        for h, cols in enumerate(heads)
    ]
    grads = jnp.concatenate(grads, axis=1).astype(jnp.bfloat16)
    term = dot(enc, grads, ((0,), (0,)))

    @pl.when(step == 0)
    def _():
        total[...] = term

    @pl.when(jnp.logical_and(step > 0, step < 3))
    def _():
        total[...] += term

    @pl.when(step == 3)
    def _():
        total[...] += term
        for zh in range(4):
            for slot in range(8):
                row = (zh * 4 + slot // 2) * 56
                for yhi in range(4):
                    col = slot % 2 * 512 + yhi * 128
                    piece = total[row : row + 56, col : col + 128]
                    term_ref[slot, zh, yhi] = piece.astype(jnp.bfloat16)


def block_spec(*shape):
    return pl.BlockSpec((1,) + shape, lambda i, core: (i,) + (0,) * len(shape))


def full_spec(*shape):
    return pl.BlockSpec(shape, lambda i, core: (0,) * len(shape))


def token_specs():
    own = pl.BlockSpec((1, BLOCK, 1024), lambda i, core: (jnp.minimum(i, 1), 0, core[0]))
    came = pl.BlockSpec((2, 1, BLOCK, 1024), lambda i, core: (0, jnp.maximum(i - 2, 0), 0, 0))
    return own, came


def pair_specs(*shape):
    rest = (0,) * len(shape)
    own = pl.BlockSpec((1,) + shape, lambda i, core: (jnp.minimum(i, 1),) + rest)
    other = pl.BlockSpec((1,) + shape, lambda i, core: (jnp.maximum(i - 2, 0),) + rest)
    return [own, other]


def key_part(core, own, other, weight, queries, cots, came):
    token, came_spec = token_specs()
    return pl.pallas_call(
        key_kernel,
        grid_spec=pltpu.PrefetchScalarGridSpec(
            num_scalar_prefetch=1,
            grid=(4,),
            in_specs=pair_specs(SPAN, 896) + [full_spec(896, 1024), token, token, came_spec],
            out_specs=[
                block_spec(SPAN, 1024),
                block_spec(8 * BLOCK, SPAN),
                full_spec(8, 4, 4, 56, 128),
            ],
            scratch_shapes=[pltpu.VMEM((896, 1024), jnp.float32)],
        ),
        out_shape=[
            jax.ShapeDtypeStruct((4, SPAN, 1024), jnp.bfloat16),
            jax.ShapeDtypeStruct((4, 8 * BLOCK, SPAN), jnp.float32),
            jax.ShapeDtypeStruct((8, 4, 4, 56, 128), jnp.bfloat16),
        ],
        compiler_params=pltpu.CompilerParams(vmem_limit_bytes=VMEM),
        cost_estimate=pl.CostEstimate(
            flops=4_000_000_000, bytes_accessed=12_000_000, transcendentals=524288
        ),
        name="key_part",
    )(core, own, other, weight, queries, cots, came)


def value_kernel(
    core_ref, own_ref, other_ref, weight_ref, key_ref, prob_ref, cot_ref, came_ref,
    mine_ref, theirs_ref,
):
    enc = pick(own_ref[0], other_ref[0])
    cot = pick(cot_ref[0], came_ref[0, 0])
    values = dot(enc, weight_ref[...], ((1,), (0,))).astype(jnp.bfloat16)
    heads = [slice(h * HEAD_DIM, (h + 1) * HEAD_DIM) for h in range(8)]
    rows = [slice(h * BLOCK, (h + 1) * BLOCK) for h in range(8)]
    probs = prob_ref[0]
    low = probs.astype(jnp.bfloat16)
    attended = [dot(low[r], values[:, c], ((1,), (0,))) for r, c in zip(rows, heads)]
    attended = jnp.concatenate(attended, axis=1).astype(jnp.bfloat16)
    prob_grad = [dot(cot[:, c], values[:, c], ((1,), (1,))) for c in heads]
    both = cot.astype(jnp.float32) * attended.astype(jnp.float32)
    row_total = [jnp.sum(both[:, c], axis=-1, keepdims=True) for c in heads]
    score_grad = SCALE * probs * (jnp.concatenate(prob_grad) - jnp.concatenate(row_total))
    score_grad = score_grad.astype(jnp.bfloat16)
    qgrad = [dot(score_grad[r], key_ref[0, :, c], ((1,), (0,))) for r, c in zip(rows, heads)]
    qgrad = jnp.concatenate(qgrad, axis=1).astype(jnp.bfloat16)
    step = pl.program_id(0)

    @pl.when(step < 2)
    def _():
        mine_ref[0, 0] = attended
        mine_ref[0, 1] = qgrad

    @pl.when(step >= 2)
    def _():
        theirs_ref[0, 0] = attended
        theirs_ref[0, 1] = qgrad


def value_part(core, own, other, weight, keys, probs, cots, came):
    token, _ = token_specs()
    came_spec = pl.BlockSpec((1, 1, BLOCK, 1024), lambda i, core: (1, jnp.maximum(i - 2, 0), 0, 0))
    return pl.pallas_call(
        value_kernel,
        grid_spec=pltpu.PrefetchScalarGridSpec(
            num_scalar_prefetch=1,
            grid=(4,),
            in_specs=pair_specs(SPAN, 896)
            + [
                full_spec(896, 1024),
                block_spec(SPAN, 1024),
                block_spec(8 * BLOCK, SPAN),
                token,
                came_spec,
            ],
            out_specs=pair_specs(2, BLOCK, 1024),
        ),
        out_shape=[jax.ShapeDtypeStruct((2, 2, BLOCK, 1024), jnp.bfloat16)] * 2,
        compiler_params=pltpu.CompilerParams(vmem_limit_bytes=VMEM),
        cost_estimate=pl.CostEstimate(
            flops=2_500_000_000, bytes_accessed=10_000_000, transcendentals=0
        ),
        name="value_part",
    )(core, own, other, weight, keys, probs, cots, came)


def body(queries, pool, slots, key_weight, value_weight, cotangent):
    core, xp = lax.axis_index("core"), lax.axis_index("xp")
    ylo, zl = lax.axis_index("ylo"), lax.axis_index("zl")
    which = core.astype(jnp.int32).reshape(1)
    bf16, f32 = jnp.bfloat16, jnp.float32

    def columns(weight, core):
        return lax.dynamic_slice(weight, (0, core * 1024 + xp * 512), (28, 512))

    weights = (key_weight, value_weight)
    mine = jnp.concatenate([columns(w, core) for w in weights], 1)
    came = swap(jnp.concatenate([columns(w, 1 - core) for w in weights], 1))
    block = copies(ordered(core == 0, mine, came, 0), 4)

    along = lax.all_to_all(block, "zh", 0, 0)
    key_z, value_z = along[:, :, :512], along[:, :, 512:]

    slots, queries, cotangent = after((slots, queries, cotangent), block)
    rows = jnp.take(pool[0], slots[0].reshape(-1), axis=0).reshape(2, SPAN, 896)
    own = jnp.stack([next_group(rows[1]), rows[0]])
    other = swap(own)
    theirs = [lax.dynamic_slice(v[0], (0, (1 - core) * 1024), (128, 1024)) for v in (queries, cotangent)]
    tokens = swap(jnp.stack(theirs)).reshape(2, 2, BLOCK, 1024)
    queries, cotangent = queries.reshape(2, BLOCK, 2048), cotangent.reshape(2, BLOCK, 2048)

    key_copies = copies(after(key_z, own), 8)
    cube = lax.all_to_all(key_copies, CUBE, 0, 0).reshape(2, 2, 2, 4, 56, 512)
    cube = jnp.concatenate([cube[:, :, 0], cube[:, :, 1]], axis=-1)
    key_whole = cube.transpose(2, 0, 1, 3, 4).reshape(896, 1024)
    value_z = after(value_z, key_copies)
    value_z = ordered(zl == 0, value_z[:, None], lax.ppermute(value_z, AXES, ODD_Z)[:, None], 1)
    value_z = value_z.reshape(8, 56, 512)
    key_whole, value_z = lax.optimization_barrier((key_whole, value_z))
    keys, probs, term = key_part(which, own, other, key_whole, queries, cotangent, tokens)

    cube = lax.all_to_all(term, CUBE, 0, 0)
    value_z = after(value_z, term)
    around = [lax.ppermute(value_z, AXES, pairs) for pairs in ODD_SQUARE]
    sums = jnp.sum(cube.astype(f32), axis=0).astype(bf16).reshape(16, 56, 128)
    by_x, by_y, by_xy = after(around, sums)
    along = lax.all_to_all(sums, ("zh", "yhi"), 0, 0)
    same = ordered(xp == 0, value_z, by_x, 2)
    across = ordered(xp == 0, by_y, by_xy, 2)
    value_whole = ordered(ylo == 0, same[:, None], across[:, None], 1).reshape(896, 1024)
    mine, theirs = value_part(which, own, other, value_whole, keys, probs, cotangent, tokens)

    done = jnp.sum(along.astype(f32), axis=0).astype(bf16).reshape(2, 1, 28, 128)
    done = jnp.broadcast_to(done, (2, 16, 28, 128)).reshape(32, 28, 128)
    pieces = lax.all_to_all(done, ("core", "xh", "xp", "yhi"), 0, 0)
    pieces = pieces.reshape(2, 2, 2, 4, 28, 128).astype(f32)
    weight_grad = jnp.sum(pieces, axis=1).transpose(3, 0, 1, 2, 4).reshape(28, 2048)

    came = swap(after(theirs, done))
    attended = ordered(core == 0, mine[:, 0], came[:, 0], 2)
    query_grad = ordered(core == 0, mine[:, 1], came[:, 1], 2)
    return attended.reshape(1, 128, 2048), query_grad.reshape(1, 128, 2048), weight_grad


def solution(mesh):
    fine = Mesh(mesh.devices.reshape(SIZES), AXES)
    by_token = P(DP, SEQ, None)
    return jax.shard_map(
        body,
        mesh=fine,
        in_specs=(
            by_token,
            P(DP, SEQ, None, None),
            by_token,
            P(DP, None),
            P(DP, None),
            by_token,
        ),
        out_specs=(by_token, by_token, P(DP, None)),
        check_vma=False,
    )
```

time: 420 us -> 167 us (0.40)
  the two profiles are of different devices: /device:TPU:22 before, /device:TPU:1 now
where the time goes in v2:
time: 167 us; the launch traced here: 166 us
  starting transfers between devices  94.2 us (56%)
  waiting for transfers between devices  26.7 us (16%)
  Pallas kernels  21.5 us (13%)
  local copies, waits for them, and re-layouts  12.5 us (7%)
  other arithmetic  10.4 us (6%)
    all_to_all x1, starting transfers between devices, body(): along = lax.all_to_all(sums, ('zh', 'yhi'), 0, 0)  23.7 us
    ppermute x3, starting transfers between devices, body(): around = [lax.ppermute(value_z, AXES, pairs) for pairs in ODD_SQUARE]  23.7 us
    ppermute x4, starting transfers between devices, swap(): return lax.ppermute(value, 'core', [(0, 1), (1, 0)])  16.8 us
    pallas_call x1, Pallas kernels, key_part(): pl.pallas_call(key_kernel, grid_spec=pltpu.PrefetchScalarGridSpec(num_sca...  13 us
    ppermute x1, waiting for transfers between devices, next_group(): return lax.ppermute(rows, SEQ, [(i - 1, i) for i in range(1, n)])  9.18 us
    pallas_call x1, Pallas kernels, value_part(): pl.pallas_call(value_kernel, grid_spec=pltpu.PrefetchScalarGridSpec(num_s...  8.51 us
    all_to_all x1, waiting for transfers between devices, body(): along = lax.all_to_all(sums, ('zh', 'yhi'), 0, 0)  7.36 us
    all_to_all x1, waiting for transfers between devices, body(): cube = lax.all_to_all(key_copies, CUBE, 0, 0).reshape(2, 2, 2, 4, 56, 512)  7.18 us
  transfers between devices with their start and end apart: 14, of which 6 were waited for; matrix products, arithmetic and copies ran while one was open for 9% of the time, Pallas kernels for 5%

profile of v2, /device:TPU:1, one launch (start us, length us, event | category | flops | bytes accessed | tf_op | source)
XLA Modules:
  0.0 166.2 jit_solution(7585899561411578841)
XLA Ops:
  0.7 0.9 constant_dynamic-slice_fusion.4
  1.6 8.8 %collective-permute-start = (bf16[28,1024]{1,0:T(8,128)(2,1)S(1)}, bf16[28,1024]{1,0:T(8,128)(2,1)S(1)}, u32[]{:S(2)}, u32[]{:S(2)}) collective-permute-start(bf16[28,1024]{1,0:T(8,128)(2,1)S(1)} %pad_maximum_fusion.2), channel_id=1, source_target_pairs={{0,1},{1,0},{2,3},{3,2},{4,5},{5,4},{6,7},{7,6},{8,9},{9,8},{10,11... | collective-permute-start | bytes 172040 | tf_op jit(solution)/shard_map/ppermute | solution.py:56
  10.4 0.9 collective-permute-done
  11.3 0.8 broadcast_in_dim.37
  12.2 0.8 reshape_squeeze.6
  12.9 0.8 reshape_squeeze.5
  13.7 4.6 %all-to-all-start = ((bf16[4,56,1024]{2,1,0:T(8,128)(2,1)}), bf16[4,56,1024]{2,1,0:T(8,128)(2,1)S(1)}, u32[]{:S(2)}, u32[]{:S(2)}) async-start(bf16[4,56,1024]{2,1,0:T(8,128)(2,1)} %broadcast_in_dim.37), calls=%async_computation | async-start | bytes 917504 | tf_op jit(solution)/shard_map/all_to_all | solution.py:249
  18.3 0.7 gather_fusion
  19.1 0.2 broadcast_select_fusion
  19.3 3.1 %collective-permute-start.1 = (bf16[256,896]{1,0:T(8,128)(2,1)S(1)}, bf16[256,896]{1,0:T(8,128)(2,1)S(1)}, u32[]{:S(2)}, u32[]{:S(2)}) collective-permute-start(bf16[256,896]{1,0:T(8,128)(2,1)S(1)} %bitcast.62), channel_id=1, source_target_pairs={{0,32},{32,64},{64,96},{96,128},{128,160},{160,192},{192,224},{224... | collective-permute-start | bytes 1376264 | tf_op jit(solution)/shard_map/ppermute | solution.py:61
  22.5 9.2 %collective-permute-done.1 = bf16[256,896]{1,0:T(8,128)(2,1)S(1)} collective-permute-done((bf16[256,896]{1,0:T(8,128)(2,1)S(1)}, bf16[256,896]{1,0:T(8,128)(2,1)S(1)}, u32[]{:S(2)}, u32[]{:S(2)}) %collective-permute-start.1) | collective-permute-done | bytes 458784 | tf_op jit(solution)/shard_map/ppermute | solution.py:61
  31.6 1.1 pad_maximum_fusion.own_ref
  32.8 1.4 broadcast_in_dim.40
  34.2 5.4 %all-to-all-start.1 = ((bf16[8,4,56,512]{3,2,1,0:T(8,128)(2,1)}), bf16[8,4,56,512]{3,2,1,0:T(8,128)(2,1)S(1)}, u32[]{:S(2)}, u32[]{:S(2)}) async-start(bf16[8,4,56,512]{3,2,1,0:T(8,128)(2,1)} %broadcast_in_dim.40), calls=%async_computation.1 | async-start | bytes 3670016 | tf_op jit(solution)/shard_map/all_to_all | solution.py:261
  39.6 3.7 %collective-permute-start.2 = (bf16[2,256,896]{2,1,0:T(8,128)(2,1)}, bf16[2,256,896]{2,1,0:T(8,128)(2,1)}, u32[]{:S(2)}, u32[]{:S(2)}) collective-permute-start(bf16[2,256,896]{2,1,0:T(8,128)(2,1)} %pad_maximum_fusion.own_ref), channel_id=1, source_target_pairs={{0,1},{1,0},{2,3},{3,2},{4,5},{5,4},{6,7},{7,6},{8,9},{9,8},{10,11... | collective-permute-start | bytes 2752520 | tf_op jit(solution)/shard_map/ppermute | solution.py:56
  43.3 1.0 constant_dynamic-slice_fusion.1
  44.3 6.0 %collective-permute-start.3 = (bf16[4,56,512]{2,1,0:T(8,128)(2,1)S(1)}, bf16[4,56,512]{2,1,0:T(8,128)(2,1)S(1)}, u32[]{:S(2)}, u32[]{:S(2)}) collective-permute-start(bf16[4,56,512]{2,1,0:T(8,128)(2,1)S(1)} %get-tuple-element.22), channel_id=1, source_target_pairs={{0,28},{1,29},{4,8},{5,9},{8,4},{9,5},{12,16},{13,17},{16,12},{17,... | collective-permute-start | bytes 688136 | tf_op jit(solution)/shard_map/ppermute | solution.py:265
  50.3 1.0 constant_dynamic-slice_fusion
  51.3 0.8 pad_maximum_fusion.1
  52.1 2.2 %collective-permute-start.4 = (bf16[2,128,1024]{2,1,0:T(8,128)(2,1)}, bf16[2,128,1024]{2,1,0:T(8,128)(2,1)}, u32[]{:S(2)}, u32[]{:S(2)}) collective-permute-start(bf16[2,128,1024]{2,1,0:T(8,128)(2,1)} %pad_maximum_fusion.1), channel_id=1, source_target_pairs={{0,1},{1,0},{2,3},{3,2},{4,5},{5,4},{6,7},{7,6},{8,9},{9,8},{10,11... | collective-permute-start | bytes 1572872 | tf_op jit(solution)/shard_map/ppermute | solution.py:56
  54.3 1.9 %collective-permute-done.3 = bf16[4,56,512]{2,1,0:T(8,128)(2,1)S(1)} collective-permute-done((bf16[4,56,512]{2,1,0:T(8,128)(2,1)S(1)}, bf16[4,56,512]{2,1,0:T(8,128)(2,1)S(1)}, u32[]{:S(2)}, u32[]{:S(2)}) %collective-permute-start.3) | collective-permute-done | bytes 229408 | tf_op jit(solution)/shard_map/ppermute | solution.py:265
  56.3 0.8 copy.39
  57.1 7.2 %all-to-all-done.1 = bf16[8,4,56,512]{3,2,1,0:T(8,128)(2,1)S(1)} async-done(((bf16[8,4,56,512]{3,2,1,0:T(8,128)(2,1)}), bf16[8,4,56,512]{3,2,1,0:T(8,128)(2,1)S(1)}, u32[]{:S(2)}, u32[]{:S(2)}) %all-to-all-start.1) | async-done | bytes 1835040 | tf_op jit(solution)/shard_map/all_to_all | solution.py:261
  64.3 0.1 slice_bitcast_fusion.1
  64.4 0.3 maximum_bitcast_fusion
  64.7 1.4 copy.38
  66.1 13.0 %key_part.1 = (bf16[4,256,1024]{2,1,0:T(8,128)(2,1)}, f32[4,512,256]{2,1,0:T(8,128)}, bf16[8,4,4,56,128]{4,3,2,1,0:T(8,128)(2,1)}) custom-call(s32[1]{0:T(128)} %bitcast.core_ref, bf16[2,256,896]{2,1,0:T(8,128)(2,1)} %pad_maximum_fusion.own_ref, bf16[2,256,896]{2,1,0:T(8,128)(2,1)} %collective-permute-done.2.other_ref, bf16[896,1024]{1,0:T(8,128)(2,1)} %bitcast.49, ...), custom_call_target="tpu_custom_call" | custom-call | flops 4000000000 | bytes 12000000 | tf_op jit(solution)/shard_map/key_part/pallas_call | solution.py:149
  79.1 3.6 %all-to-all-start.2 = ((bf16[8,4,4,56,128]{4,3,2,1,0:T(8,128)(2,1)}), bf16[8,4,4,56,128]{4,3,2,1,0:T(8,128)(2,1)S(1)}, u32[]{:S(2)}, u32[]{:S(2)}) async-start(bf16[8,4,4,56,128]{4,3,2,1,0:T(8,128)(2,1)} %get-tuple-element.27), calls=%async_computation.2 | async-start | bytes 3670016 | tf_op jit(solution)/shard_map/all_to_all | solution.py:270
  82.7 7.9 %collective-permute-start.7 = (bf16[8,56,512]{2,1,0:T(8,128)(2,1)}, bf16[8,56,512]{2,1,0:T(8,128)(2,1)}, u32[]{:S(2)}, u32[]{:S(2)}) collective-permute-start(bf16[8,56,512]{2,1,0:T(8,128)(2,1)} %bitcast.51), channel_id=1, source_target_pairs={{0,482},{1,483},{4,486},{5,487},{8,490},{9,491},{12,494},{13,495},... | collective-permute-start | bytes 1376264 | tf_op jit(solution)/shard_map/ppermute | solution.py:272
  90.7 12.8 %collective-permute-start.6 = (bf16[8,56,512]{2,1,0:T(8,128)(2,1)}, bf16[8,56,512]{2,1,0:T(8,128)(2,1)}, u32[]{:S(2)}, u32[]{:S(2)}) collective-permute-start(bf16[8,56,512]{2,1,0:T(8,128)(2,1)} %bitcast.52), channel_id=1, source_target_pairs={{0,386},{1,387},{4,390},{5,391},{8,394},{9,395},{12,398},{13,399},... | collective-permute-start | bytes 1376264 | tf_op jit(solution)/shard_map/ppermute | solution.py:272
  103.4 3.0 %collective-permute-start.5 = (bf16[8,56,512]{2,1,0:T(8,128)(2,1)}, bf16[8,56,512]{2,1,0:T(8,128)(2,1)}, u32[]{:S(2)}, u32[]{:S(2)}) collective-permute-start(bf16[8,56,512]{2,1,0:T(8,128)(2,1)} %bitcast.53), channel_id=1, source_target_pairs={{0,96},{1,97},{4,100},{5,101},{8,104},{9,105},{12,108},{13,109},{1... | collective-permute-start | bytes 1376264 | tf_op jit(solution)/shard_map/ppermute | solution.py:272
  106.4 1.0 reduce_sum.33
  107.4 23.7 %all-to-all-start.3 = ((bf16[16,56,128]{2,1,0:T(8,128)(2,1)}), bf16[16,56,128]{2,1,0:T(8,128)(2,1)S(1)}, u32[]{:S(2)}, u32[]{:S(2)}) async-start(bf16[16,56,128]{2,1,0:T(8,128)(2,1)} %bitcast.18), calls=%async_computation.3 | async-start | bytes 458752 | tf_op jit(solution)/shard_map/all_to_all | solution.py:275
  131.2 1.7 %fusion = bf16[8,1,56,1024]{3,2,1,0:T(8,128)(2,1)S(1)} fusion(bf16[8,1,56,512]{3,2,0,1:T(8,128)(2,1)} %bitcast.19, bf16[8,1,56,512]{3,2,0,1:T(8,128)(2,1)} %bitcast.54, pred[]{:T(512)S(6)} %eq.17), kind=kLoop, calls=%fused_computation.7 | loop fusion | flops 4128768 | bytes 1835009 | tf_op jit(solution)/shard_map/jit(_where)/select_n | solution.py:65
  132.9 1.8 %maximum_select_fusion.1 = bf16[8,1,56,1024]{3,2,1,0:T(8,128)(2,1)S(1)} fusion(bf16[8,1,56,512]{3,2,1,0:T(8,128)(2,1)} %bitcast.23, bf16[8,1,56,512]{3,2,1,0:T(8,128)(2,1)} %bitcast.22, pred[]{:T(512)S(6)} %eq.17), kind=kLoop, calls=%fused_computation.9 | loop fusion | flops 4128768 | bytes 1835009 | tf_op jit(solution)/shard_map/jit(_where)/select_n | solution.py:65
  134.7 1.4 maximum_select_fusion
  136.1 7.4 %all-to-all-done.3 = bf16[16,56,128]{2,1,0:T(8,128)(2,1)S(1)} async-done(((bf16[16,56,128]{2,1,0:T(8,128)(2,1)}), bf16[16,56,128]{2,1,0:T(8,128)(2,1)S(1)}, u32[]{:S(2)}, u32[]{:S(2)}) %all-to-all-start.3) | async-done | bytes 229408 | tf_op jit(solution)/shard_map/all_to_all | solution.py:275
  143.5 0.7 broadcast_in_dim.44
  144.3 7.2 %all-to-all-start.4 = ((bf16[32,28,128]{2,1,0:T(8,128)(2,1)}), bf16[32,28,128]{2,1,0:T(8,128)(2,1)S(1)}, u32[]{:S(2)}, u32[]{:S(2)}) async-start(bf16[32,28,128]{2,1,0:T(8,128)(2,1)} %bitcast.26), calls=%async_computation.4 | async-start | bytes 524288 | tf_op jit(solution)/shard_map/all_to_all | solution.py:283
  151.5 8.5 %value_part.1 = (bf16[2,2,64,1024]{3,2,1,0:T(8,128)(2,1)}, bf16[2,2,64,1024]{3,2,1,0:T(8,128)(2,1)}) custom-call(s32[1]{0:T(128)} %bitcast.core_ref, bf16[2,256,896]{2,1,0:T(8,128)(2,1)} %pad_maximum_fusion.own_ref, bf16[2,256,896]{2,1,0:T(8,128)(2,1)} %collective-permute-done.2.other_ref, bf16[896,1024]{1,0:T(8,128)(2,1)} %bitcast.50, ...), custom_call_target="tpu_custom_call" | custom-call | flops 2500000000 | bytes 10000000 | tf_op jit(solution)/shard_map/value_part/pallas_call | solution.py:211
  160.0 2.1 %collective-permute-start.8 = (bf16[2,2,64,1024]{3,2,1,0:T(8,128)(2,1)}, bf16[2,2,64,1024]{3,2,1,0:T(8,128)(2,1)S(1)}, u32[]{:S(2)}, u32[]{:S(2)}) collective-permute-start(bf16[2,2,64,1024]{3,2,1,0:T(8,128)(2,1)} %get-tuple-element.36), channel_id=1, source_target_pairs={{0,1},{1,0},{2,3},{3,2},{4,5},{5,4},{6,7},{7,6},{8,9},{9,8},{10,11... | collective-permute-start | bytes 1572872 | tf_op jit(solution)/shard_map/ppermute | solution.py:56
  162.1 1.1 fusion.3
  163.2 0.1 all-to-all-done.4
  163.3 0.1 copy.42
  163.4 0.1 convert_reduce_fusion
  163.6 0.8 reshape.358
  164.4 0.9 maximum_select_fusion.3
  165.3 0.9 maximum_select_fusion.2
  (21 shorter events, 0.4 us)
Async XLA Ops:
  0.6 17.7 %copy-start = (bf16[1,6,128,896]{3,2,1,0:T(8,128)(2,1)S(1)}, bf16[1,6,128,896]{3,2,1,0:T(8,128)(2,1)}, u32[]{:S(2)}) copy-start(bf16[1,6,128,896]{3,2,1,0:T(8,128)(2,1)} %param.7) | copy-start | bytes 4128772
  1.6 9.7 %collective-permute-start = (bf16[28,1024]{1,0:T(8,128)(2,1)S(1)}, bf16[28,1024]{1,0:T(8,128)(2,1)S(1)}, u32[]{:S(2)}, u32[]{:S(2)}) collective-permute-start(bf16[28,1024]{1,0:T(8,128)(2,1)S(1)} %pad_maximum_fusion.2), channel_id=1, source_target_pairs={{0,1},{1,0},{2,3},{3,2},{4,5},{5,4},{6,7},{7,6},{8,9},{9,8},{10,11... | collective-permute-start | bytes 172040 | tf_op jit(solution)/shard_map/ppermute | solution.py:56
  13.7 19.1 %all-to-all-start = ((bf16[4,56,1024]{2,1,0:T(8,128)(2,1)}), bf16[4,56,1024]{2,1,0:T(8,128)(2,1)S(1)}, u32[]{:S(2)}, u32[]{:S(2)}) async-start(bf16[4,56,1024]{2,1,0:T(8,128)(2,1)} %broadcast_in_dim.37), calls=%async_computation | async-start | bytes 917504 | tf_op jit(solution)/shard_map/all_to_all | solution.py:249
  19.3 12.3 %collective-permute-start.1 = (bf16[256,896]{1,0:T(8,128)(2,1)S(1)}, bf16[256,896]{1,0:T(8,128)(2,1)S(1)}, u32[]{:S(2)}, u32[]{:S(2)}) collective-permute-start(bf16[256,896]{1,0:T(8,128)(2,1)S(1)} %bitcast.62), channel_id=1, source_target_pairs={{0,32},{32,64},{64,96},{96,128},{128,160},{160,192},{192,224},{224... | collective-permute-start | bytes 1376264 | tf_op jit(solution)/shard_map/ppermute | solution.py:61
  34.2 30.1 %all-to-all-start.1 = ((bf16[8,4,56,512]{3,2,1,0:T(8,128)(2,1)}), bf16[8,4,56,512]{3,2,1,0:T(8,128)(2,1)S(1)}, u32[]{:S(2)}, u32[]{:S(2)}) async-start(bf16[8,4,56,512]{3,2,1,0:T(8,128)(2,1)} %broadcast_in_dim.40), calls=%async_computation.1 | async-start | bytes 3670016 | tf_op jit(solution)/shard_map/all_to_all | solution.py:261
  39.6 26.5 %collective-permute-start.2 = (bf16[2,256,896]{2,1,0:T(8,128)(2,1)}, bf16[2,256,896]{2,1,0:T(8,128)(2,1)}, u32[]{:S(2)}, u32[]{:S(2)}) collective-permute-start(bf16[2,256,896]{2,1,0:T(8,128)(2,1)} %pad_maximum_fusion.own_ref), channel_id=1, source_target_pairs={{0,1},{1,0},{2,3},{3,2},{4,5},{5,4},{6,7},{7,6},{8,9},{9,8},{10,11... | collective-permute-start | bytes 2752520 | tf_op jit(solution)/shard_map/ppermute | solution.py:56
  44.3 12.0 %collective-permute-start.3 = (bf16[4,56,512]{2,1,0:T(8,128)(2,1)S(1)}, bf16[4,56,512]{2,1,0:T(8,128)(2,1)S(1)}, u32[]{:S(2)}, u32[]{:S(2)}) collective-permute-start(bf16[4,56,512]{2,1,0:T(8,128)(2,1)S(1)} %get-tuple-element.22), channel_id=1, source_target_pairs={{0,28},{1,29},{4,8},{5,9},{8,4},{9,5},{12,16},{13,17},{16,12},{17,... | collective-permute-start | bytes 688136 | tf_op jit(solution)/shard_map/ppermute | solution.py:265
  52.1 14.0 %collective-permute-start.4 = (bf16[2,128,1024]{2,1,0:T(8,128)(2,1)}, bf16[2,128,1024]{2,1,0:T(8,128)(2,1)}, u32[]{:S(2)}, u32[]{:S(2)}) collective-permute-start(bf16[2,128,1024]{2,1,0:T(8,128)(2,1)} %pad_maximum_fusion.1), channel_id=1, source_target_pairs={{0,1},{1,0},{2,3},{3,2},{4,5},{5,4},{6,7},{7,6},{8,9},{9,8},{10,11... | collective-permute-start | bytes 1572872 | tf_op jit(solution)/shard_map/ppermute | solution.py:56
  79.1 27.3 %all-to-all-start.2 = ((bf16[8,4,4,56,128]{4,3,2,1,0:T(8,128)(2,1)}), bf16[8,4,4,56,128]{4,3,2,1,0:T(8,128)(2,1)S(1)}, u32[]{:S(2)}, u32[]{:S(2)}) async-start(bf16[8,4,4,56,128]{4,3,2,1,0:T(8,128)(2,1)} %get-tuple-element.27), calls=%async_computation.2 | async-start | bytes 3670016 | tf_op jit(solution)/shard_map/all_to_all | solution.py:270
  82.7 48.4 %collective-permute-start.7 = (bf16[8,56,512]{2,1,0:T(8,128)(2,1)}, bf16[8,56,512]{2,1,0:T(8,128)(2,1)}, u32[]{:S(2)}, u32[]{:S(2)}) collective-permute-start(bf16[8,56,512]{2,1,0:T(8,128)(2,1)} %bitcast.51), channel_id=1, source_target_pairs={{0,482},{1,483},{4,486},{5,487},{8,490},{9,491},{12,494},{13,495},... | collective-permute-start | bytes 1376264 | tf_op jit(solution)/shard_map/ppermute | solution.py:272
  90.7 40.5 %collective-permute-start.6 = (bf16[8,56,512]{2,1,0:T(8,128)(2,1)}, bf16[8,56,512]{2,1,0:T(8,128)(2,1)}, u32[]{:S(2)}, u32[]{:S(2)}) collective-permute-start(bf16[8,56,512]{2,1,0:T(8,128)(2,1)} %bitcast.52), channel_id=1, source_target_pairs={{0,386},{1,387},{4,390},{5,391},{8,394},{9,395},{12,398},{13,399},... | collective-permute-start | bytes 1376264 | tf_op jit(solution)/shard_map/ppermute | solution.py:272
  103.4 27.7 %collective-permute-start.5 = (bf16[8,56,512]{2,1,0:T(8,128)(2,1)}, bf16[8,56,512]{2,1,0:T(8,128)(2,1)}, u32[]{:S(2)}, u32[]{:S(2)}) collective-permute-start(bf16[8,56,512]{2,1,0:T(8,128)(2,1)} %bitcast.53), channel_id=1, source_target_pairs={{0,96},{1,97},{4,100},{5,101},{8,104},{9,105},{12,108},{13,109},{1... | collective-permute-start | bytes 1376264 | tf_op jit(solution)/shard_map/ppermute | solution.py:272
  107.4 36.1 %all-to-all-start.3 = ((bf16[16,56,128]{2,1,0:T(8,128)(2,1)}), bf16[16,56,128]{2,1,0:T(8,128)(2,1)S(1)}, u32[]{:S(2)}, u32[]{:S(2)}) async-start(bf16[16,56,128]{2,1,0:T(8,128)(2,1)} %bitcast.18), calls=%async_computation.3 | async-start | bytes 458752 | tf_op jit(solution)/shard_map/all_to_all | solution.py:275
  144.3 19.0 %all-to-all-start.4 = ((bf16[32,28,128]{2,1,0:T(8,128)(2,1)}), bf16[32,28,128]{2,1,0:T(8,128)(2,1)S(1)}, u32[]{:S(2)}, u32[]{:S(2)}) async-start(bf16[32,28,128]{2,1,0:T(8,128)(2,1)} %bitcast.26), calls=%async_computation.4 | async-start | bytes 524288 | tf_op jit(solution)/shard_map/all_to_all | solution.py:283
  160.0 4.4 %collective-permute-start.8 = (bf16[2,2,64,1024]{3,2,1,0:T(8,128)(2,1)}, bf16[2,2,64,1024]{3,2,1,0:T(8,128)(2,1)S(1)}, u32[]{:S(2)}, u32[]{:S(2)}) collective-permute-start(bf16[2,2,64,1024]{3,2,1,0:T(8,128)(2,1)} %get-tuple-element.36), channel_id=1, source_target_pairs={{0,1},{1,0},{2,3},{3,2},{4,5},{5,4},{6,7},{7,6},{8,9},{9,8},{10,11... | collective-permute-start | bytes 1572872 | tf_op jit(solution)/shard_map/ppermute | solution.py:56

commit v3 on v2

v3 whole, which is shorter than its diff:
```python
import math

import jax
import jax.numpy as jnp
from jax import lax
from jax.experimental import pallas as pl
from jax.experimental.pallas import tpu as pltpu
from jax.sharding import Mesh
from jax.sharding import PartitionSpec as P

HEAD_DIM = 128
BLOCK = 64
SPAN = 256
SCALE = 1.0 / math.sqrt(HEAD_DIM)

AXES = ("yhi", "xh", "xp", "zh", "zl", "ylo", "core")
SIZES = (4, 2, 2, 4, 2, 2, 2)
SEQ = ("yhi", "xh", "xp")
DP = ("zh", "zl", "ylo", "core")
CUBE = ("zl", "ylo", "xp")
VMEM = 60 * 1024 * 1024


def place(x, y, z, core):
    return (((y // 2 * 4 + x) * 8 + z) * 2 + y % 2) * 2 + core


def odd_square(dx, dy):
    return [
        (
            place(x, y, z, core),
            place((x + dx * (2 * (x % 2) - 1)) % 4, (y + dy * (2 * (y % 2) - 1)) % 8, z, core),
        )
        for x in range(4)
        for y in range(8)
        for z in range(8)
        for core in range(2)
    ]


ODD_SQUARE = [odd_square(1, 0), odd_square(0, 1), odd_square(1, 1)]
ODD_Z = [
    (place(x, y, z, core), place(x, y, (z + 2 * (z % 2) - 1) % 8, core))
    for x in range(4)
    for y in range(8)
    for z in range(8)
    for core in range(2)
]


def after(value, token):
    return lax.optimization_barrier((value, token))[0]


def swap(value):
    return lax.ppermute(value, "core", [(0, 1), (1, 0)])


def next_group(rows):
    n = 16
    return lax.ppermute(rows, SEQ, [(i - 1, i) for i in range(1, n)])


def ordered(first, own, other, axis):
    return jnp.where(
        first, jnp.concatenate([own, other], axis), jnp.concatenate([other, own], axis)
    )


def copies(value, count):
    return jnp.broadcast_to(value[None], (count,) + value.shape)


def dot(a, b, dims):
    return lax.dot_general(a, b, (dims, ((), ())), preferred_element_type=jnp.float32)


def in_rows(pieces):
    return jnp.concatenate([p.astype(jnp.float32) for p in pieces]).astype(jnp.bfloat16)


def project(own_ref, other_ref, weight):
    both = [dot(ref[...], weight, ((1,), (0,))) for ref in (own_ref, other_ref)]
    return jnp.concatenate([x.astype(jnp.bfloat16) for x in both])


PAIRS = [(block, slice(h * HEAD_DIM, (h + 1) * HEAD_DIM)) for block in range(4) for h in range(2)]


def rows_of(block):
    return slice(block * SPAN, (block + 1) * SPAN)


def token_rows(own_ref, came_ref, kind):
    tiles = [own_ref[0], own_ref[1], came_ref[kind, 0], came_ref[kind, 1]]
    return [tiles[block][:, cols] for block, cols in PAIRS]


def side_by_side(tiles):
    return jnp.concatenate([jnp.concatenate(tiles[i : i + 2], axis=1) for i in range(0, 8, 2)])


def key_kernel(
    where_ref, own_ref, other_ref, weight_ref, query_ref, cot_ref, came_ref,
    key_ref, prob_ref, term_ref, turned,
):
    @pl.when(pl.program_id(0) == 0)
    def _():
        turned[:, :512] = own_ref[...].T
        turned[:, 512:] = other_ref[...].T

    weight = in_rows(
        [weight_ref[zl, ylo, 0, zh] for zh in range(4) for zl in range(2) for ylo in range(2)]
    )
    keys = project(own_ref, other_ref, weight)
    key_ref[...] = keys
    query = token_rows(query_ref, came_ref, 0)
    cot = token_rows(cot_ref, came_ref, 1)
    scores = [
        dot(q, keys[rows_of(block), cols], ((1,), (1,))) for q, (block, cols) in zip(query, PAIRS)
    ]
    scores = jnp.concatenate(scores) * SCALE
    weights = jnp.exp(scores - jnp.max(scores, axis=-1, keepdims=True))
    probs = weights * (1.0 / jnp.sum(weights, axis=-1, keepdims=True))
    low = probs.astype(jnp.bfloat16)
    prob_ref[0] = low
    grads = [dot(low[i * BLOCK : (i + 1) * BLOCK], cot[i], ((0,), (0,))) for i in range(8)]
    grads = side_by_side([x.astype(jnp.bfloat16) for x in grads])
    term = dot(turned[...], grads, ((1,), (0,))).astype(jnp.float32)
    for zh in range(4):
        for slot in range(4):
            row = (zh * 4 + slot) * 56
            for half in range(2):
                piece = term[row : row + 56, half * 128 : (half + 1) * 128]
                term_ref[slot, 0, zh, 0, half] = piece.astype(jnp.bfloat16)


def value_kernel(
    where_ref, own_ref, other_ref, here_ref, across_ref, key_ref, prob_ref,
    cot_ref, came_ref, att_ref, qgrad_ref, theirs_ref,
):
    odd = where_ref[1] == 1
    here, across = here_ref[...], across_ref[...]
    first, second = jnp.where(odd, across, here), jnp.where(odd, here, across)
    weight = in_rows([half[z] for z in range(8) for half in (first, second)])
    values = project(own_ref, other_ref, weight)
    low = prob_ref[0]
    cot = token_rows(cot_ref, came_ref, 0)
    low_tiles = [low[i * BLOCK : (i + 1) * BLOCK] for i in range(8)]
    value_tiles = [values[rows_of(block), cols] for block, cols in PAIRS]
    attended = [
        dot(p, v, ((1,), (0,))).astype(jnp.bfloat16) for p, v in zip(low_tiles, value_tiles)
    ]
    prob_grad = [dot(g, v, ((1,), (1,))) for g, v in zip(cot, value_tiles)]
    both = jnp.concatenate(cot).astype(jnp.float32) * jnp.concatenate(attended).astype(jnp.float32)
    row_total = jnp.sum(both, axis=-1, keepdims=True)
    score_grad = SCALE * low.astype(jnp.float32) * (jnp.concatenate(prob_grad) - row_total)
    score_grad = score_grad.astype(jnp.bfloat16)
    query_grad = [
        dot(score_grad[i * BLOCK : (i + 1) * BLOCK], key_ref[rows_of(block), cols], ((1,), (0,)))
        for i, (block, cols) in enumerate(PAIRS)
    ]
    for i, (block, cols) in enumerate(PAIRS):
        qgrad = query_grad[i].astype(jnp.bfloat16)
        if block < 2:
            att_ref[block, :, cols] = attended[i]
            qgrad_ref[block, :, cols] = qgrad
        else:
            theirs_ref[0, block - 2, :, cols] = attended[i]
            theirs_ref[1, block - 2, :, cols] = qgrad


def full_spec(*shape):
    return pl.BlockSpec(shape, lambda j, where: (0,) * len(shape))


def columns_spec(*shape):
    return pl.BlockSpec(shape, lambda j, where: (0,) * (len(shape) - 1) + (j,))


def half_spec(*shape):
    return pl.BlockSpec(shape, lambda j, where: (0,) * (len(shape) - 1) + (j % 2,))


def own_tokens():
    return pl.BlockSpec((2, BLOCK, 256), lambda j, where: (0, 0, where[0] * 4 + j))


def prob_spec():
    return pl.BlockSpec((1, 512, SPAN), lambda j, where: (j, 0, 0))


PARAMS = pltpu.CompilerParams(vmem_limit_bytes=VMEM)


def key_part(where, own, other, weight, queries, cots, came):
    return pl.pallas_call(
        key_kernel,
        grid_spec=pltpu.PrefetchScalarGridSpec(
            num_scalar_prefetch=1,
            grid=(4,),
            in_specs=[
                full_spec(512, 896),
                full_spec(512, 896),
                pl.BlockSpec(
                    (2, 2, 1, 4, 56, 256), lambda j, where: (0, 0, j // 2, 0, 0, j % 2)
                ),
                own_tokens(),
                own_tokens(),
                columns_spec(2, 2, BLOCK, 256),
            ],
            out_specs=[
                columns_spec(1024, 256),
                prob_spec(),
                pl.BlockSpec(
                    (4, 1, 4, 1, 2, 56, 128), lambda j, where: (0, j // 2, 0, j % 2, 0, 0, 0)
                ),
            ],
            scratch_shapes=[pltpu.VMEM((896, 1024), jnp.bfloat16)],
        ),
        out_shape=[
            jax.ShapeDtypeStruct((1024, 1024), jnp.bfloat16),
            jax.ShapeDtypeStruct((4, 512, SPAN), jnp.bfloat16),
            jax.ShapeDtypeStruct((4, 2, 4, 2, 2, 56, 128), jnp.bfloat16),
        ],
        compiler_params=PARAMS,
        cost_estimate=pl.CostEstimate(
            flops=4_000_000_000, bytes_accessed=10_000_000, transcendentals=524288
        ),
        name="key_part",
    )(where, own, other, weight, queries, cots, came)


def value_part(far, where, own, other, weights, keys, probs, cots, came):
    def at(i, where):
        return 2 * (where[2] ^ far) + i

    return pl.pallas_call(
        value_kernel,
        grid_spec=pltpu.PrefetchScalarGridSpec(
            num_scalar_prefetch=1,
            grid=(2,),
            in_specs=[full_spec(512, 896), full_spec(512, 896)]
            + [columns_spec(8, 56, 256)] * 2
            + [
                pl.BlockSpec((1024, 256), lambda i, where: (0, at(i, where))),
                pl.BlockSpec((1, 512, SPAN), lambda i, where: (at(i, where), 0, 0)),
                pl.BlockSpec((2, BLOCK, 256), lambda i, where: (0, 0, where[0] * 4 + at(i, where))),
                pl.BlockSpec((1, 2, BLOCK, 256), lambda i, where: (1, 0, 0, at(i, where))),
            ],
            out_specs=[columns_spec(2, BLOCK, 256)] * 2 + [columns_spec(2, 2, BLOCK, 256)],
        ),
        out_shape=[
            jax.ShapeDtypeStruct((2, BLOCK, 512), jnp.bfloat16),
            jax.ShapeDtypeStruct((2, BLOCK, 512), jnp.bfloat16),
            jax.ShapeDtypeStruct((2, 2, BLOCK, 512), jnp.bfloat16),
        ],
        compiler_params=PARAMS,
        cost_estimate=pl.CostEstimate(
            flops=1_250_000_000, bytes_accessed=6_000_000, transcendentals=0
        ),
        name="value_part",
    )(where, own, other, *weights, keys, probs, cots, came)


def copy_kernel(slots_ref, pool_ref, rows_ref):
    rows_ref[...] = pool_ref[0, 0]


def chosen(slots, pool, block):
    return pl.pallas_call(
        copy_kernel,
        grid_spec=pltpu.PrefetchScalarGridSpec(
            num_scalar_prefetch=1,
            grid=(2,),
            in_specs=[
                pl.BlockSpec((1, 1, 128, 896), lambda i, slots: (0, slots[0, block, i], 0, 0))
            ],
            out_specs=pl.BlockSpec((128, 896), lambda i, slots: (i, 0)),
        ),
        out_shape=jax.ShapeDtypeStruct((SPAN, 896), jnp.bfloat16),
        compiler_params=PARAMS,
        cost_estimate=pl.CostEstimate(flops=0, bytes_accessed=900_000, transcendentals=0),
        name="chosen",
    )(slots, pool)


def body(queries, pool, slots, key_weight, value_weight, cotangent):
    core, xp = lax.axis_index("core"), lax.axis_index("xp")
    ylo, zl = lax.axis_index("ylo"), lax.axis_index("zl")
    where = jnp.stack([core, ylo, xp]).astype(jnp.int32)
    bf16, f32 = jnp.bfloat16, jnp.float32

    def columns(weight, core):
        return lax.dynamic_slice(weight, (0, core * 1024 + xp * 512), (28, 512))

    last = chosen(slots, pool, 1)
    arrived = next_group(last)
    weights = after((key_weight, value_weight), last)
    mine = jnp.concatenate([columns(w, core) for w in weights], 1)
    came = swap(jnp.concatenate([columns(w, 1 - core) for w in weights], 1))
    block = copies(ordered(core == 0, mine, came, 0), 4)

    along = lax.all_to_all(block, "zh", 0, 0)
    key_z, value_z = along[:, :, :512], along[:, :, 512:]

    slots = after(slots, (block, arrived))
    first = chosen(slots, pool, 0)
    own = jnp.concatenate([arrived, first])
    queries, cotangent = after((queries, cotangent), arrived)
    theirs = [lax.dynamic_slice(v[0], (0, (1 - core) * 1024), (128, 1024)) for v in (queries, cotangent)]
    tokens = swap(jnp.stack(theirs)).reshape(2, 2, BLOCK, 1024)
    queries, cotangent = queries.reshape(2, BLOCK, 2048), cotangent.reshape(2, BLOCK, 2048)

    key_copies = copies(after(key_z, (first, tokens)), 8)
    cube = lax.all_to_all(key_copies, CUBE, 0, 0).reshape(2, 2, 2, 4, 56, 512)
    value_z = after(value_z, key_copies)
    value_z = ordered(zl == 0, value_z[:, None], lax.ppermute(value_z, AXES, ODD_Z)[:, None], 1)
    value_z = value_z.reshape(8, 56, 512)
    other = swap(after(own, value_z))
    around = [lax.ppermute(value_z, AXES, pairs) for pairs in ODD_SQUARE[:2]]
    cube, value_z = lax.optimization_barrier((cube, value_z))
    keys, probs, term = key_part(where, own, other, cube, queries, cotangent, tokens)

    term, around = lax.optimization_barrier((term, around))
    cube = lax.all_to_all(term.reshape(8, 16, 56, 128), CUBE, 0, 0)
    around.append(lax.ppermute(after(value_z, term), AXES, ODD_SQUARE[2]))
    by_x, by_y, by_xy = around
    rest = (keys, probs, cotangent, tokens)
    near = value_part(0, where, own, other, (value_z, by_y), *rest)
    near_came = swap(near[2])
    sums = jnp.sum(cube.astype(f32), axis=0).astype(bf16)
    sums, near, near_came = lax.optimization_barrier((sums, near, near_came))
    along = lax.all_to_all(sums, ("zh", "yhi"), 0, 0)
    by_x, by_xy = after((by_x, by_xy), sums)
    far = value_part(1, where, own, other, (by_x, by_xy), *rest)
    along = after(along, far)
    done = jnp.sum(along.astype(f32), axis=0).astype(bf16).reshape(2, 1, 28, 128)
    done = jnp.broadcast_to(done, (2, 16, 28, 128)).reshape(32, 28, 128)
    pieces = lax.all_to_all(done, ("core", "xh", "xp", "yhi"), 0, 0)
    far_came = swap(far[2])
    near, far, near_came, far_came = after((near, far, near_came, far_came), done)

    def outputs(kind):
        mine = ordered(xp == 0, near[kind], far[kind], 2)
        came = ordered(xp == 0, near_came[kind], far_came[kind], 2)
        return ordered(core == 0, mine, came, 2).reshape(1, 128, 2048)

    pieces = pieces.reshape(2, 2, 2, 4, 28, 128).astype(f32)
    weight_grad = jnp.sum(pieces, axis=1).transpose(3, 0, 1, 2, 4).reshape(28, 2048)
    return outputs(0), outputs(1), weight_grad


def solution(mesh):
    fine = Mesh(mesh.devices.reshape(SIZES), AXES)
    by_token = P(DP, SEQ, None)
    return jax.shard_map(
        body,
        mesh=fine,
        in_specs=(
            by_token,
            P(DP, SEQ, None, None),
            by_token,
            P(DP, None),
            P(DP, None),
            by_token,
        ),
        out_specs=(by_token, by_token, P(DP, None)),
        check_vma=False,
    )
```

time: 167 us -> 164 us (0.982)
  Pallas kernels: 21.5 us -> 29.5 us
  other arithmetic: 10.4 us -> 4.21 us
  local copies, waits for them, and re-layouts: 12.5 us -> 6.71 us
  waiting for transfers between devices: 26.7 us -> 30.7 us
  starting transfers between devices: 94.2 us -> 91 us
    all_to_all x1, waiting for transfers between devices: 0.13 us -> 9.65 us  [body(): pieces = lax.all_to_all(done, ('core', 'xh', 'xp', 'yhi'), 0, 0)]
    ppermute x1, waiting for transfers between devices: 9.18 us -> 0.01 us  [next_group(): return lax.ppermute(rows, SEQ, [(i - 1, i) for i in range(1, n)])]
    all_to_all x1, waiting for transfers between devices: 0.01 us -> 7.45 us  [body(): cube = lax.all_to_all(term.reshape(8, 16, 56, 128), CUBE, 0, 0)]
    all_to_all x1, waiting for transfers between devices: 7.18 us -> 0.01 us  [body(): cube = lax.all_to_all(key_copies, CUBE, 0, 0).reshape(2, 2, 2, 4, 56, 512)]
    all_to_all x1, starting transfers between devices: 23.7 us -> 17.1 us  [body(): along = lax.all_to_all(sums, ('zh', 'yhi'), 0, 0)]
    all_to_all x1, waiting for transfers between devices: 0.01 us -> 6.15 us  [body(): along = lax.all_to_all(block, 'zh', 0, 0)]
    all_to_all x1, waiting for transfers between devices: 7.36 us -> 2.04 us  [body(): along = lax.all_to_all(sums, ('zh', 'yhi'), 0, 0)]
    pallas_call x0 -> x2, Pallas kernels: none -> 5.07 us  [chosen(): pl.pallas_call(copy_kernel, grid_spec=pltpu.PrefetchScalarGridSpec(num_sc...]
  transfers between devices with their start and end apart: 14 -> 15, of which waited for: 6 -> 6; matrix products, arithmetic and copies ran while one was open for 9% -> 4% of each run, Pallas kernels for 5% -> 16%
where the time goes in v3:
time: 164 us; the launch traced here: 163 us
  starting transfers between devices  91 us (55%)
  waiting for transfers between devices  30.7 us (19%)
  Pallas kernels  29.5 us (18%)
  local copies, waits for them, and re-layouts  6.71 us (4%)
  other arithmetic  4.21 us (3%)
    ppermute x5, starting transfers between devices, swap(): return lax.ppermute(value, 'core', [(0, 1), (1, 0)])  20.2 us
    all_to_all x1, starting transfers between devices, body(): along = lax.all_to_all(sums, ('zh', 'yhi'), 0, 0)  17.1 us
    ppermute x2, starting transfers between devices, body(): around = [lax.ppermute(value_z, AXES, pairs) for pairs in ODD_SQUARE[:2]]  12.8 us
    pallas_call x1, Pallas kernels, key_part(): pl.pallas_call(key_kernel, grid_spec=pltpu.PrefetchScalarGridSpec(num_sca...  12.3 us
    pallas_call x2, Pallas kernels, value_part(): pl.pallas_call(value_kernel, grid_spec=pltpu.PrefetchScalarGridSpec(num_s...  12.1 us
    all_to_all x1, waiting for transfers between devices, body(): pieces = lax.all_to_all(done, ('core', 'xh', 'xp', 'yhi'), 0, 0)  9.65 us
    ppermute x1, starting transfers between devices, body(): around.append(lax.ppermute(after(value_z, term), AXES, ODD_SQUARE[2]))  8.8 us
    all_to_all x1, starting transfers between devices, body(): cube = lax.all_to_all(key_copies, CUBE, 0, 0).reshape(2, 2, 2, 4, 56, 512)  7.97 us
  transfers between devices with their start and end apart: 15, of which 6 were waited for; matrix products, arithmetic and copies ran while one was open for 4% of the time, Pallas kernels for 16%

profile of v3, /device:TPU:1, one launch (start us, length us, event | category | flops | bytes accessed | tf_op | source)
XLA Modules:
  0.0 163.3 jit_solution(13304834704816619407)
XLA Ops:
  0.7 0.0 copy-start.2
  0.7 2.6 %chosen.2 = bf16[256,896]{1,0:T(8,128)(2,1)} custom-call(s32[1,2,2]{2,1,0:T(2,128)} %slots_ref.2, bf16[1,6,128,896]{3,2,1,0:T(8,128)(2,1)} %pool_ref.3), custom_call_target="tpu_custom_call" | custom-call | bytes 900000 | tf_op jit(solution)/shard_map/chosen/pallas_call | solution.py:271
  3.3 4.0 %collective-permute-start = (bf16[256,896]{1,0:T(8,128)(2,1)}, bf16[256,896]{1,0:T(8,128)(2,1)S(1)}, u32[]{:S(2)}, u32[]{:S(2)}) collective-permute-start(bf16[256,896]{1,0:T(8,128)(2,1)} %chosen.2), channel_id=1, source_target_pairs={{0,32},{32,64},{64,96},{96,128},{128,160},{160,192},{192,224},{224... | collective-permute-start | bytes 1376264 | tf_op jit(solution)/shard_map/ppermute | solution.py:61
  7.3 6.1 %collective-permute-start.1 = (bf16[28,1024]{1,0:T(8,128)(2,1)S(1)}, bf16[28,1024]{1,0:T(8,128)(2,1)S(1)}, u32[]{:S(2)}, u32[]{:S(2)}) collective-permute-start(bf16[28,1024]{1,0:T(8,128)(2,1)S(1)} %pad_maximum_fusion.2), channel_id=1, source_target_pairs={{0,1},{1,0},{2,3},{3,2},{4,5},{5,4},{6,7},{7,6},{8,9},{9,8},{10,11... | collective-permute-start | bytes 172040 | tf_op jit(solution)/shard_map/ppermute | solution.py:56
  13.5 0.9 collective-permute-done.1
  14.4 0.8 broadcast_in_dim.12
  15.2 6.7 %all-to-all-start = ((bf16[4,56,1024]{2,1,0:T(8,128)(2,1)}), bf16[4,56,1024]{2,1,0:T(8,128)(2,1)S(1)}, u32[]{:S(2)}, u32[]{:S(2)}) async-start(bf16[4,56,1024]{2,1,0:T(8,128)(2,1)} %broadcast_in_dim.12), calls=%async_computation | async-start | bytes 917504 | tf_op jit(solution)/shard_map/all_to_all | solution.py:304
  22.0 0.1 pad_maximum_fusion.1
  22.1 2.5 %collective-permute-start.2 = (bf16[2,128,1024]{2,1,0:T(8,128)(2,1)S(1)}, bf16[2,128,1024]{2,1,0:T(8,128)(2,1)S(1)}, u32[]{:S(2)}, u32[]{:S(2)}) collective-permute-start(bf16[2,128,1024]{2,1,0:T(8,128)(2,1)S(1)} %pad_maximum_fusion.1), channel_id=1, source_target_pairs={{0,1},{1,0},{2,3},{3,2},{4,5},{5,4},{6,7},{7,6},{8,9},{9,8},{10,11... | collective-permute-start | bytes 1572872 | tf_op jit(solution)/shard_map/ppermute | solution.py:56
  24.6 2.5 %chosen.3 = bf16[256,896]{1,0:T(8,128)(2,1)} custom-call(s32[1,2,2]{2,1,0:T(2,128)} %slots_ref.2, bf16[1,6,128,896]{3,2,1,0:T(8,128)(2,1)} %pool_ref.3), custom_call_target="tpu_custom_call" | custom-call | bytes 900000 | tf_op jit(solution)/shard_map/chosen/pallas_call | solution.py:271
  27.1 6.2 %all-to-all-done = bf16[4,56,1024]{2,1,0:T(8,128)(2,1)S(1)} async-done(((bf16[4,56,1024]{2,1,0:T(8,128)(2,1)}), bf16[4,56,1024]{2,1,0:T(8,128)(2,1)S(1)}, u32[]{:S(2)}, u32[]{:S(2)}) %all-to-all-start) | async-done | bytes 458784 | tf_op jit(solution)/shard_map/all_to_all | solution.py:304
  33.3 0.0 copy-start.3
  33.3 1.4 broadcast_in_dim.26
  34.8 8.0 %all-to-all-start.1 = ((bf16[8,4,56,512]{3,2,1,0:T(8,128)(2,1)}), bf16[8,4,56,512]{3,2,1,0:T(8,128)(2,1)}, u32[]{:S(2)}, u32[]{:S(2)}) async-start(bf16[8,4,56,512]{3,2,1,0:T(8,128)(2,1)} %broadcast_in_dim.26), calls=%async_computation.1 | async-start | bytes 3670016 | tf_op jit(solution)/shard_map/all_to_all | solution.py:316
  42.7 3.9 %collective-permute-start.3 = (bf16[4,56,512]{2,1,0:T(8,128)(2,1)S(1)}, bf16[4,56,512]{2,1,0:T(8,128)(2,1)S(1)}, u32[]{:S(2)}, u32[]{:S(2)}) collective-permute-start(bf16[4,56,512]{2,1,0:T(8,128)(2,1)S(1)} %get-tuple-element.45), channel_id=1, source_target_pairs={{0,28},{1,29},{4,8},{5,9},{8,4},{9,5},{12,16},{13,17},{16,12},{17,... | collective-permute-start | bytes 688136 | tf_op jit(solution)/shard_map/ppermute | solution.py:318
  46.6 0.1 pad_maximum_fusion.own_ref
  46.7 4.5 %collective-permute-done.3 = bf16[4,56,512]{2,1,0:T(8,128)(2,1)S(1)} collective-permute-done((bf16[4,56,512]{2,1,0:T(8,128)(2,1)S(1)}, bf16[4,56,512]{2,1,0:T(8,128)(2,1)S(1)}, u32[]{:S(2)}, u32[]{:S(2)}) %collective-permute-start.3) | collective-permute-done | bytes 229408 | tf_op jit(solution)/shard_map/ppermute | solution.py:318
  51.3 4.5 %collective-permute-start.4 = (bf16[512,896]{1,0:T(8,128)(2,1)S(1)}, bf16[512,896]{1,0:T(8,128)(2,1)S(1)}, u32[]{:S(2)}, u32[]{:S(2)}) collective-permute-start(bf16[512,896]{1,0:T(8,128)(2,1)S(1)} %pad_maximum_fusion.own_ref), channel_id=1, source_target_pairs={{0,1},{1,0},{2,3},{3,2},{4,5},{5,4},{6,7},{7,6},{8,9},{9,8},{10,11... | collective-permute-start | bytes 2752520 | tf_op jit(solution)/shard_map/ppermute | solution.py:56
  55.8 10.8 %collective-permute-start.6 = (bf16[8,56,512]{2,1,0:T(8,128)(2,1)S(1)}, bf16[8,56,512]{2,1,0:T(8,128)(2,1)S(1)}, u32[]{:S(2)}, u32[]{:S(2)}) collective-permute-start(bf16[8,56,512]{2,1,0:T(8,128)(2,1)S(1)} %bitcast.39), channel_id=1, source_target_pairs={{0,386},{1,387},{4,390},{5,391},{8,394},{9,395},{12,398},{13,399},... | collective-permute-start | bytes 1376264 | tf_op jit(solution)/shard_map/ppermute | solution.py:321
  66.7 1.9 %collective-permute-start.5 = (bf16[8,56,512]{2,1,0:T(8,128)(2,1)S(1)}, bf16[8,56,512]{2,1,0:T(8,128)(2,1)S(1)}, u32[]{:S(2)}, u32[]{:S(2)}) collective-permute-start(bf16[8,56,512]{2,1,0:T(8,128)(2,1)S(1)} %bitcast.40), channel_id=1, source_target_pairs={{0,96},{1,97},{4,100},{5,101},{8,104},{9,105},{12,108},{13,109},{1... | collective-permute-start | bytes 1376264 | tf_op jit(solution)/shard_map/ppermute | solution.py:321
  68.6 0.6 pad_add_fusion.where_ref
  69.3 1.0 copy-done.1
  70.2 12.3 %key_part.1 = (bf16[1024,1024]{1,0:T(8,128)(2,1)}, bf16[4,512,256]{2,1,0:T(8,128)(2,1)}, bf16[4,2,4,2,2,56,128]{6,5,4,3,2,1,0:T(8,128)(2,1)}) custom-call(s32[3]{0:T(128)} %pad_add_fusion.where_ref, bf16[512,896]{1,0:T(8,128)(2,1)} %copy-done, bf16[512,896]{1,0:T(8,128)(2,1)} %copy-done.1, bf16[2,2,2,4,56,512]{5,4,3,2,1,0:T(8,128)(2,1)} %bitcast.7.weight_ref, ...), custom_call_target="tpu_custom_call" | custom-call | flops 4000000000 | bytes 10000000 | tf_op jit(solution)/shard_map/key_part/pallas_call | solution.py:197
  82.6 0.7 copy-done.8
  83.3 0.1 copy-done.6
  83.5 3.6 %all-to-all-start.2 = ((bf16[8,16,56,128]{3,2,1,0:T(8,128)(2,1)}), bf16[8,16,56,128]{3,2,1,0:T(8,128)(2,1)S(1)}, u32[]{:S(2)}, u32[]{:S(2)}) async-start(bf16[8,16,56,128]{3,2,1,0:T(8,128)(2,1)} %bitcast.38), calls=%async_computation.2 | async-start | bytes 3670016 | tf_op jit(solution)/shard_map/all_to_all | solution.py:326
  87.1 8.8 %collective-permute-start.8 = (bf16[8,56,512]{2,1,0:T(8,128)(2,1)S(1)}, bf16[8,56,512]{2,1,0:T(8,128)(2,1)S(1)}, u32[]{:S(2)}, u32[]{:S(2)}) collective-permute-start(bf16[8,56,512]{2,1,0:T(8,128)(2,1)S(1)} %bitcast.41), channel_id=1, source_target_pairs={{0,482},{1,483},{4,486},{5,487},{8,490},{9,491},{12,494},{13,495},... | collective-permute-start | bytes 1376264 | tf_op jit(solution)/shard_map/ppermute | solution.py:327
  95.9 6.1 %value_part.2 = (bf16[2,64,512]{2,1,0:T(8,128)(2,1)}, bf16[2,64,512]{2,1,0:T(8,128)(2,1)}, bf16[2,2,64,512]{3,2,1,0:T(8,128)(2,1)}) custom-call(s32[3]{0:T(128)} %pad_add_fusion.where_ref, bf16[512,896]{1,0:T(8,128)(2,1)} %copy-done, bf16[512,896]{1,0:T(8,128)(2,1)} %copy-done.1, bf16[8,56,512]{2,1,0:T(8,128)(2,1)} %bitcast.42, ...), custom_call_target="tpu_custom_call" | custom-call | flops 1250000000 | bytes 6000000 | tf_op jit(solution)/shard_map/value_part/pallas_call | solution.py:238
  102.0 3.0 %collective-permute-start.7 = (bf16[2,2,64,512]{3,2,1,0:T(8,128)(2,1)}, bf16[2,2,64,512]{3,2,1,0:T(8,128)(2,1)S(1)}, u32[]{:S(2)}, u32[]{:S(2)}) collective-permute-start(bf16[2,2,64,512]{3,2,1,0:T(8,128)(2,1)} %get-tuple-element.56), channel_id=1, source_target_pairs={{0,1},{1,0},{2,3},{3,2},{4,5},{5,4},{6,7},{7,6},{8,9},{9,8},{10,11... | collective-permute-start | bytes 786440 | tf_op jit(solution)/shard_map/ppermute | solution.py:56
  105.0 7.5 %all-to-all-done.2 = bf16[8,16,56,128]{3,2,1,0:T(8,128)(2,1)S(1)} async-done(((bf16[8,16,56,128]{3,2,1,0:T(8,128)(2,1)}), bf16[8,16,56,128]{3,2,1,0:T(8,128)(2,1)S(1)}, u32[]{:S(2)}, u32[]{:S(2)}) %all-to-all-start.2) | async-done | bytes 1835040 | tf_op jit(solution)/shard_map/all_to_all | solution.py:326
  112.5 1.0 reduce_sum.33
  113.5 17.1 %all-to-all-start.3 = ((bf16[16,56,128]{2,1,0:T(8,128)(2,1)}), bf16[16,56,128]{2,1,0:T(8,128)(2,1)S(1)}, u32[]{:S(2)}, u32[]{:S(2)}) async-start(bf16[16,56,128]{2,1,0:T(8,128)(2,1)} %reduce_sum.33), calls=%async_computation.3 | async-start | bytes 458752 | tf_op jit(solution)/shard_map/all_to_all | solution.py:334
  130.6 0.8 copy-done.7
  131.4 6.1 %value_part.3 = (bf16[2,64,512]{2,1,0:T(8,128)(2,1)}, bf16[2,64,512]{2,1,0:T(8,128)(2,1)}, bf16[2,2,64,512]{3,2,1,0:T(8,128)(2,1)}) custom-call(s32[3]{0:T(128)} %pad_add_fusion.where_ref, bf16[512,896]{1,0:T(8,128)(2,1)} %copy-done, bf16[512,896]{1,0:T(8,128)(2,1)} %copy-done.1, bf16[8,56,512]{2,1,0:T(8,128)(2,1)} %copy-done.6, ...), custom_call_target="tpu_custom_call" | custom-call | flops 1250000000 | bytes 6000000 | tf_op jit(solution)/shard_map/value_part/pallas_call | solution.py:238
  137.5 4.0 %collective-permute-start.9 = (bf16[2,2,64,512]{3,2,1,0:T(8,128)(2,1)}, bf16[2,2,64,512]{3,2,1,0:T(8,128)(2,1)S(1)}, u32[]{:S(2)}, u32[]{:S(2)}) collective-permute-start(bf16[2,2,64,512]{3,2,1,0:T(8,128)(2,1)} %get-tuple-element.66), channel_id=1, source_target_pairs={{0,1},{1,0},{2,3},{3,2},{4,5},{5,4},{6,7},{7,6},{8,9},{9,8},{10,11... | collective-permute-start | bytes 786440 | tf_op jit(solution)/shard_map/ppermute | solution.py:56
  141.5 2.0 %all-to-all-done.3 = bf16[16,56,128]{2,1,0:T(8,128)(2,1)S(1)} async-done(((bf16[16,56,128]{2,1,0:T(8,128)(2,1)}), bf16[16,56,128]{2,1,0:T(8,128)(2,1)S(1)}, u32[]{:S(2)}, u32[]{:S(2)}) %all-to-all-start.3) | async-done | bytes 229408 | tf_op jit(solution)/shard_map/all_to_all | solution.py:334
  143.6 0.7 broadcast_in_dim.30
  144.3 6.0 %all-to-all-start.4 = ((bf16[32,28,128]{2,1,0:T(8,128)(2,1)}), bf16[32,28,128]{2,1,0:T(8,128)(2,1)S(1)}, u32[]{:S(2)}, u32[]{:S(2)}) async-start(bf16[32,28,128]{2,1,0:T(8,128)(2,1)} %bitcast.11), calls=%async_computation.4 | async-start | bytes 524288 | tf_op jit(solution)/shard_map/all_to_all | solution.py:340
  150.4 0.1 fusion
  150.5 0.1 fusion.2
  150.6 0.1 fusion.3
  150.7 0.1 fusion.1
  150.8 0.9 maximum_select_fusion.1
  151.7 0.9 maximum_select_fusion
  152.6 9.7 %all-to-all-done.4 = bf16[32,28,128]{2,1,0:T(8,128)(2,1)S(1)} async-done(((bf16[32,28,128]{2,1,0:T(8,128)(2,1)}), bf16[32,28,128]{2,1,0:T(8,128)(2,1)S(1)}, u32[]{:S(2)}, u32[]{:S(2)}) %all-to-all-start.4) | async-done | bytes 229408 | tf_op jit(solution)/shard_map/all_to_all | solution.py:340
  162.3 0.1 copy.15
  162.4 0.1 convert_reduce_fusion
  162.5 0.8 reshape.421
  (45 shorter events, 0.4 us)
Async XLA Ops:
  0.6 6.6 %copy-start.14 = (bf16[28,2048]{1,0:T(8,128)(2,1)S(1)}, bf16[28,2048]{1,0:T(8,128)(2,1)}, u32[]{:S(2)}) copy-start(bf16[28,2048]{1,0:T(8,128)(2,1)} %param.10) | copy-start | bytes 344068
  0.6 6.6 %copy-start.15 = (bf16[28,2048]{1,0:T(8,128)(2,1)S(1)}, bf16[28,2048]{1,0:T(8,128)(2,1)}, u32[]{:S(2)}) copy-start(bf16[28,2048]{1,0:T(8,128)(2,1)} %param.9) | copy-start | bytes 344068
  0.7 21.3 %copy-start.2 = (bf16[1,128,2048]{2,1,0:T(8,128)(2,1)S(1)}, bf16[1,128,2048]{2,1,0:T(8,128)(2,1)}, u32[]{:S(2)}) copy-start(bf16[1,128,2048]{2,1,0:T(8,128)(2,1)} %param.11) | copy-start | bytes 1572868
  0.7 21.3 %copy-start.13 = (bf16[1,128,2048]{2,1,0:T(8,128)(2,1)S(1)}, bf16[1,128,2048]{2,1,0:T(8,128)(2,1)}, u32[]{:S(2)}) copy-start(bf16[1,128,2048]{2,1,0:T(8,128)(2,1)} %param.6) | copy-start | bytes 1572868
  3.3 18.7 %collective-permute-start = (bf16[256,896]{1,0:T(8,128)(2,1)}, bf16[256,896]{1,0:T(8,128)(2,1)S(1)}, u32[]{:S(2)}, u32[]{:S(2)}) collective-permute-start(bf16[256,896]{1,0:T(8,128)(2,1)} %chosen.2), channel_id=1, source_target_pairs={{0,32},{32,64},{64,96},{96,128},{128,160},{160,192},{192,224},{224... | collective-permute-start | bytes 1376264 | tf_op jit(solution)/shard_map/ppermute | solution.py:61
  7.3 7.0 %collective-permute-start.1 = (bf16[28,1024]{1,0:T(8,128)(2,1)S(1)}, bf16[28,1024]{1,0:T(8,128)(2,1)S(1)}, u32[]{:S(2)}, u32[]{:S(2)}) collective-permute-start(bf16[28,1024]{1,0:T(8,128)(2,1)S(1)} %pad_maximum_fusion.2), channel_id=1, source_target_pairs={{0,1},{1,0},{2,3},{3,2},{4,5},{5,4},{6,7},{7,6},{8,9},{9,8},{10,11... | collective-permute-start | bytes 172040 | tf_op jit(solution)/shard_map/ppermute | solution.py:56
  15.2 18.0 %all-to-all-start = ((bf16[4,56,1024]{2,1,0:T(8,128)(2,1)}), bf16[4,56,1024]{2,1,0:T(8,128)(2,1)S(1)}, u32[]{:S(2)}, u32[]{:S(2)}) async-start(bf16[4,56,1024]{2,1,0:T(8,128)(2,1)} %broadcast_in_dim.12), calls=%async_computation | async-start | bytes 917504 | tf_op jit(solution)/shard_map/all_to_all | solution.py:304
  22.1 11.2 %collective-permute-start.2 = (bf16[2,128,1024]{2,1,0:T(8,128)(2,1)S(1)}, bf16[2,128,1024]{2,1,0:T(8,128)(2,1)S(1)}, u32[]{:S(2)}, u32[]{:S(2)}) collective-permute-start(bf16[2,128,1024]{2,1,0:T(8,128)(2,1)S(1)} %pad_maximum_fusion.1), channel_id=1, source_target_pairs={{0,1},{1,0},{2,3},{3,2},{4,5},{5,4},{6,7},{7,6},{8,9},{9,8},{10,11... | collective-permute-start | bytes 1572872 | tf_op jit(solution)/shard_map/ppermute | solution.py:56
  33.3 1.4 copy-start.3
  34.8 11.9 %copy-start.4 = (bf16[256,896]{1,0:T(8,128)(2,1)S(1)}, bf16[256,896]{1,0:T(8,128)(2,1)}, u32[]{:S(2)}) copy-start(bf16[256,896]{1,0:T(8,128)(2,1)} %chosen.3) | copy-start | bytes 1376260
  34.8 34.5 %all-to-all-start.1 = ((bf16[8,4,56,512]{3,2,1,0:T(8,128)(2,1)}), bf16[8,4,56,512]{3,2,1,0:T(8,128)(2,1)}, u32[]{:S(2)}, u32[]{:S(2)}) async-start(bf16[8,4,56,512]{3,2,1,0:T(8,128)(2,1)} %broadcast_in_dim.26), calls=%async_computation.1 | async-start | bytes 3670016 | tf_op jit(solution)/shard_map/all_to_all | solution.py:316
  42.7 8.5 %collective-permute-start.3 = (bf16[4,56,512]{2,1,0:T(8,128)(2,1)S(1)}, bf16[4,56,512]{2,1,0:T(8,128)(2,1)S(1)}, u32[]{:S(2)}, u32[]{:S(2)}) collective-permute-start(bf16[4,56,512]{2,1,0:T(8,128)(2,1)S(1)} %get-tuple-element.45), channel_id=1, source_target_pairs={{0,28},{1,29},{4,8},{5,9},{8,4},{9,5},{12,16},{13,17},{16,12},{17,... | collective-permute-start | bytes 688136 | tf_op jit(solution)/shard_map/ppermute | solution.py:318
  46.7 22.5 %copy-start = (bf16[512,896]{1,0:T(8,128)(2,1)}, bf16[512,896]{1,0:T(8,128)(2,1)S(1)}, u32[]{:S(2)}) copy-start(bf16[512,896]{1,0:T(8,128)(2,1)S(1)} %pad_maximum_fusion.own_ref) | copy-start | bytes 2752516
  51.3 35.8 %copy-start.5 = (bf16[4,2,56,512]{3,2,1,0:T(8,128)(2,1)}, bf16[4,2,56,512]{3,2,1,0:T(8,128)(2,1)S(1)}, u32[]{:S(2)}) copy-start(bf16[4,2,56,512]{3,2,1,0:T(8,128)(2,1)S(1)} %maximum_select_fusion.2) | copy-start | bytes 1376260
  51.3 17.9 %collective-permute-start.4 = (bf16[512,896]{1,0:T(8,128)(2,1)S(1)}, bf16[512,896]{1,0:T(8,128)(2,1)S(1)}, u32[]{:S(2)}, u32[]{:S(2)}) collective-permute-start(bf16[512,896]{1,0:T(8,128)(2,1)S(1)} %pad_maximum_fusion.own_ref), channel_id=1, source_target_pairs={{0,1},{1,0},{2,3},{3,2},{4,5},{5,4},{6,7},{7,6},{8,9},{9,8},{10,11... | collective-permute-start | bytes 2752520 | tf_op jit(solution)/shard_map/ppermute | solution.py:56
  55.8 26.7 %collective-permute-start.6 = (bf16[8,56,512]{2,1,0:T(8,128)(2,1)S(1)}, bf16[8,56,512]{2,1,0:T(8,128)(2,1)S(1)}, u32[]{:S(2)}, u32[]{:S(2)}) collective-permute-start(bf16[8,56,512]{2,1,0:T(8,128)(2,1)S(1)} %bitcast.39), channel_id=1, source_target_pairs={{0,386},{1,387},{4,390},{5,391},{8,394},{9,395},{12,398},{13,399},... | collective-permute-start | bytes 1376264 | tf_op jit(solution)/shard_map/ppermute | solution.py:321
  66.7 15.9 %collective-permute-start.5 = (bf16[8,56,512]{2,1,0:T(8,128)(2,1)S(1)}, bf16[8,56,512]{2,1,0:T(8,128)(2,1)S(1)}, u32[]{:S(2)}, u32[]{:S(2)}) collective-permute-start(bf16[8,56,512]{2,1,0:T(8,128)(2,1)S(1)} %bitcast.40), channel_id=1, source_target_pairs={{0,96},{1,97},{4,100},{5,101},{8,104},{9,105},{12,108},{13,109},{1... | collective-permute-start | bytes 1376264 | tf_op jit(solution)/shard_map/ppermute | solution.py:321
  69.2 1.0 copy-start.1
  82.6 0.8 copy-start.8
  82.6 0.9 copy-start.6
  83.5 29.0 %all-to-all-start.2 = ((bf16[8,16,56,128]{3,2,1,0:T(8,128)(2,1)}), bf16[8,16,56,128]{3,2,1,0:T(8,128)(2,1)S(1)}, u32[]{:S(2)}, u32[]{:S(2)}) async-start(bf16[8,16,56,128]{3,2,1,0:T(8,128)(2,1)} %bitcast.38), calls=%async_computation.2 | async-start | bytes 3670016 | tf_op jit(solution)/shard_map/all_to_all | solution.py:326
  87.1 43.5 %collective-permute-start.8 = (bf16[8,56,512]{2,1,0:T(8,128)(2,1)S(1)}, bf16[8,56,512]{2,1,0:T(8,128)(2,1)S(1)}, u32[]{:S(2)}, u32[]{:S(2)}) collective-permute-start(bf16[8,56,512]{2,1,0:T(8,128)(2,1)S(1)} %bitcast.41), channel_id=1, source_target_pairs={{0,482},{1,483},{4,486},{5,487},{8,490},{9,491},{12,494},{13,495},... | collective-permute-start | bytes 1376264 | tf_op jit(solution)/shard_map/ppermute | solution.py:327
  102.0 11.5 %collective-permute-start.7 = (bf16[2,2,64,512]{3,2,1,0:T(8,128)(2,1)}, bf16[2,2,64,512]{3,2,1,0:T(8,128)(2,1)S(1)}, u32[]{:S(2)}, u32[]{:S(2)}) collective-permute-start(bf16[2,2,64,512]{3,2,1,0:T(8,128)(2,1)} %get-tuple-element.56), channel_id=1, source_target_pairs={{0,1},{1,0},{2,3},{3,2},{4,5},{5,4},{6,7},{7,6},{8,9},{9,8},{10,11... | collective-permute-start | bytes 786440 | tf_op jit(solution)/shard_map/ppermute | solution.py:56
  113.5 30.0 %all-to-all-start.3 = ((bf16[16,56,128]{2,1,0:T(8,128)(2,1)}), bf16[16,56,128]{2,1,0:T(8,128)(2,1)S(1)}, u32[]{:S(2)}, u32[]{:S(2)}) async-start(bf16[16,56,128]{2,1,0:T(8,128)(2,1)} %reduce_sum.33), calls=%async_computation.3 | async-start | bytes 458752 | tf_op jit(solution)/shard_map/all_to_all | solution.py:334
  130.6 0.8 copy-start.7
  137.4 12.9 %copy-start.10 = (bf16[2,64,512]{2,1,0:T(8,128)(2,1)S(1)}, bf16[2,64,512]{2,1,0:T(8,128)(2,1)}, u32[]{:S(2)}) copy-start(bf16[2,64,512]{2,1,0:T(8,128)(2,1)} %get-tuple-element.69) | copy-start | bytes 393220
  137.5 12.9 %copy-start.12 = (bf16[2,64,512]{2,1,0:T(8,128)(2,1)S(1)}, bf16[2,64,512]{2,1,0:T(8,128)(2,1)}, u32[]{:S(2)}) copy-start(bf16[2,64,512]{2,1,0:T(8,128)(2,1)} %get-tuple-element.70) | copy-start | bytes 393220
  137.5 13.0 %copy-start.9 = (bf16[2,64,512]{2,1,0:T(8,128)(2,1)S(1)}, bf16[2,64,512]{2,1,0:T(8,128)(2,1)}, u32[]{:S(2)}) copy-start(bf16[2,64,512]{2,1,0:T(8,128)(2,1)} %get-tuple-element.73) | copy-start | bytes 393220
  137.5 13.0 %copy-start.11 = (bf16[2,64,512]{2,1,0:T(8,128)(2,1)S(1)}, bf16[2,64,512]{2,1,0:T(8,128)(2,1)}, u32[]{:S(2)}) copy-start(bf16[2,64,512]{2,1,0:T(8,128)(2,1)} %get-tuple-element.74) | copy-start | bytes 393220
  137.5 12.8 %collective-permute-start.9 = (bf16[2,2,64,512]{3,2,1,0:T(8,128)(2,1)}, bf16[2,2,64,512]{3,2,1,0:T(8,128)(2,1)S(1)}, u32[]{:S(2)}, u32[]{:S(2)}) collective-permute-start(bf16[2,2,64,512]{3,2,1,0:T(8,128)(2,1)} %get-tuple-element.66), channel_id=1, source_target_pairs={{0,1},{1,0},{2,3},{3,2},{4,5},{5,4},{6,7},{7,6},{8,9},{9,8},{10,11... | collective-permute-start | bytes 786440 | tf_op jit(solution)/shard_map/ppermute | solution.py:56
  144.3 18.0 %all-to-all-start.4 = ((bf16[32,28,128]{2,1,0:T(8,128)(2,1)}), bf16[32,28,128]{2,1,0:T(8,128)(2,1)S(1)}, u32[]{:S(2)}, u32[]{:S(2)}) async-start(bf16[32,28,128]{2,1,0:T(8,128)(2,1)} %bitcast.11), calls=%async_computation.4 | async-start | bytes 524288 | tf_op jit(solution)/shard_map/all_to_all | solution.py:340
